TPU v7x, 32 devices: a whole 2x2x4 slice. The times are simulated.
32 devices in a mesh: visit: 4 (over z), sky: 8 (over y, x, core).
Axes of the slice: x: 2, y: 2, z: 4, core: 2. Of those that a mesh axis runs over, the one named last changes fastest.
Arguments:
- cutouts: float32 [64, 512, 512], P(('visit', 'sky')), may hold values from -6 to 6
- vert_taps: float32 [64, 16, 21], P(('visit', 'sky')), may hold values from -1.25 to 1.25
- horiz_taps: float32 [64, 16, 21], P(('visit', 'sky')), may hold values from -1.25 to 1.25
- field_coeffs: float32 [64, 4, 16], P(('visit', 'sky')), may hold values from -1.5 to 1.5
- exposure_weight: float32 [64], P(('visit', 'sky')), may hold values from 0.2 to 2
- dest_owner: int32 [64, 16, 1], P(('visit', 'sky')), may hold values from 0 to 31; in each aligned block of 32 rows (0 to 31, 32 to 63, ..., all dimensions but the last counted through in order) at most 2 rows name the same one
- dest_column: int32 [64, 16], P(('visit', 'sky')), may hold values from 0 to 3
- shift_index: int32 [64, 16], P(('visit', 'sky')), may hold values from 0 to 15
- threshold_level: int32 [32, 4], replicated, may hold values from 1 to 4
Outputs:
- sky_template: float32 [4096, 512], P(('visit', 'sky'))
- difference: float32 [64, 512, 512], P(('visit', 'sky'))
Inputs may be any that keep to these rules, and one draw needn't show every extreme that they name: `dest_owner`: among the blocks of the cutouts of one device no owner is named more than 2 times, a bound that some block reaches.
All inputs are finite; a program needn't handle non-finite values.
Results may differ from a plain program's by a relative error of at most 0.0084.
Values may be sent and summed in bfloat16 or wider, within the bound.
A program may use at most 64 MiB of HBM per device.

v0:
```python
import jax
import jax.numpy as jnp
from jax import lax
from jax.sharding import PartitionSpec as P

BLOCK = 128
PW = 4
SWEEPS = 2


highest = lax.Precision.HIGHEST
spline_taps = (0.0625, 0.25, 0.375, 0.25, 0.0625)
fine_tau = 0.04
coarse_tau = 0.02
reach_rows = 6


def extended(shard, sides, width):
    for axis, dim in sides:
        peers, length = (lax.axis_size(axis), shard.shape[dim])
        up = [(i, (i + 1) % peers) for i in range(peers - 1)]
        down = [(j, i) for i, j in up]
        last = lax.slice_in_dim(shard, length - width, length, axis=dim)
        leading = lax.slice_in_dim(shard, 0, width, axis=dim)
        before = lax.ppermute(last, axis, up)
        after = lax.ppermute(leading, axis, down)
        shard = jnp.concatenate([before, shard, after], axis=dim)
    return shard


def band_matrix(kernel_taps, tile_width):
    margin = (kernel_taps.shape[1] - 1) // 2
    lag_table = jnp.arange(tile_width + 2 * margin)[:, None] - jnp.arange(tile_width)[None, :]
    one_hot = (lag_table[:, :, None] == jnp.arange(kernel_taps.shape[1])[None, None, :]).astype(
        jnp.float32
    )
    return jnp.einsum(
        "kt,mnt->kmn", kernel_taps.astype(jnp.float32), one_hot, precision=highest
    ).astype(jnp.bfloat16)


def convolve_shift(bundle):
    cutout, vertical, horizontal, coeffs, shifts = bundle
    margin = (vertical.shape[1] - 1) // 2
    cut_side = cutout.shape[0]
    tile_count = cut_side // BLOCK
    window_rows = BLOCK + 2 * margin
    padded = jnp.pad(cutout.astype(jnp.bfloat16), margin)
    across = band_matrix(horizontal.astype(jnp.bfloat16), BLOCK)
    downward = band_matrix(vertical.astype(jnp.bfloat16), BLOCK).transpose(0, 2, 1)
    windows = jnp.stack(
        [
            padded[:, column_tile * BLOCK : column_tile * BLOCK + window_rows]
            for column_tile in range(tile_count)
        ]
    )
    col_pos = (jnp.arange(cut_side).astype(jnp.float32) + 0.5) / cut_side - 0.5

    def row_tile(tile_number):
        window = lax.dynamic_slice_in_dim(windows, tile_number * BLOCK, window_rows, 1)
        smeared = jnp.einsum("tmj,kjn->kmtn", window, across, preferred_element_type=jnp.float32)
        smeared = smeared.astype(jnp.bfloat16).reshape(across.shape[0], window_rows, cut_side)
        stacked = jnp.einsum("knm,kmc->knc", downward, smeared, preferred_element_type=jnp.float32)
        basis_parts = jnp.einsum("jk,knc->jnc", coeffs, stacked, precision=highest)
        row_pos = (
            (tile_number * BLOCK + jnp.arange(BLOCK)).astype(jnp.float32) + 0.5
        ) / cut_side - 0.5
        row_pos = row_pos[:, None]
        return (
            basis_parts[0]
            + row_pos * basis_parts[1]
            + col_pos[None, :] * basis_parts[2]
            + row_pos * col_pos[None, :] * basis_parts[3]
        )

    convolved = lax.map(row_tile, jnp.arange(tile_count)).reshape(cut_side, cut_side)
    padded_conv = jnp.pad(convolved, ((0, 1), (0, 1)))
    col_frac = (((shifts % 4).astype(jnp.float32) + 0.5) / 4.0).reshape(
        tile_count, 1, tile_count, 1
    )
    row_frac = (((shifts // 4).astype(jnp.float32) + 0.5) / 4.0).reshape(
        tile_count, 1, tile_count, 1
    )

    def on_grid(raster):
        return raster.reshape(tile_count, BLOCK, tile_count, BLOCK)

    result = (1.0 - row_frac) * (1.0 - col_frac) * on_grid(convolved)
    result = result + (1.0 - row_frac) * col_frac * on_grid(padded_conv[:-1, 1:])
    result = result + row_frac * (1.0 - col_frac) * on_grid(padded_conv[1:, :-1])
    result = result + row_frac * col_frac * on_grid(padded_conv[1:, 1:])
    return result.transpose(0, 2, 1, 3).reshape(tile_count * tile_count, BLOCK, BLOCK)


def smooth_rows(raster, dilation):
    kept_rows = raster.shape[0] - 4 * dilation
    summed = spline_taps[0] * raster[0:kept_rows]
    for offset in range(1, 5):
        summed = (
            summed + spline_taps[offset] * raster[offset * dilation : offset * dilation + kept_rows]
        )
    return summed


def smooth_cols(raster, dilation):
    col_count = raster.shape[1]
    padded = jnp.pad(raster, ((0, 0), (2 * dilation, 2 * dilation)))
    summed = spline_taps[0] * padded[:, 0:col_count]
    for offset in range(1, 5):
        summed = (
            summed
            + spline_taps[offset] * padded[:, offset * dilation : offset * dilation + col_count]
        )
    return summed


def shrink(detail, limit):
    return detail - jnp.clip(detail, -limit, limit)


def level_map(first_row, row_count, levels):
    owner_rows = jnp.clip((first_row + jnp.arange(row_count)) // BLOCK, 0, levels.shape[0] - 1)
    one_hot = (owner_rows[:, None] == jnp.arange(levels.shape[0])[None, :]).astype(jnp.float32)
    per_row = jnp.dot(one_hot, levels, precision=highest)
    return jnp.repeat(per_row, BLOCK, axis=1)


def sweep(wide, first_row, levels, sky_rows):
    row_count = wide.shape[0]
    positions = first_row + jnp.arange(row_count)
    inside = ((positions >= 0) & (positions < sky_rows)).astype(jnp.float32)[:, None]
    coarse_zero = wide * inside
    coarse_one = smooth_cols(smooth_rows(coarse_zero, 1), 1) * inside[2 : row_count - 2]
    coarse_two = smooth_cols(smooth_rows(coarse_one, 2), 2)
    kept_rows = row_count - 12
    detail_fine = coarse_zero[6 : 6 + kept_rows] - coarse_one[4 : 4 + kept_rows]
    detail_coarse = coarse_one[4 : 4 + kept_rows] - coarse_two
    limits = level_map(first_row + 6, kept_rows, levels)
    return (
        coarse_two
        + shrink(detail_fine, fine_tau * limits)
        + shrink(detail_coarse, coarse_tau * limits)
    )


def shards(
    cutouts,
    vert_taps,
    horiz_taps,
    field_coeffs,
    exposure_weight,
    dest_owner,
    dest_column,
    shift_index,
    threshold_level,
):
    exposures_here = cutouts.shape[0]
    cut_side = cutouts.shape[1]
    tile_count = cut_side // BLOCK
    blocks_each = tile_count * tile_count
    visit_count = lax.axis_size("visit")
    sky_count = lax.axis_size("sky")
    devices = visit_count * sky_count
    device_rows = exposures_here * blocks_each
    capacity = max(2, 2 * device_rows // devices)
    shifted = lax.map(convolve_shift, (cutouts, vert_taps, horiz_taps, field_coeffs, shift_index))
    shifted = shifted.reshape(device_rows, BLOCK, BLOCK)
    owners = dest_owner.reshape(device_rows)
    columns = dest_column.reshape(device_rows)
    same_owner = owners[:, None] == owners[None, :]
    earlier = jnp.arange(device_rows)[None, :] < jnp.arange(device_rows)[:, None]
    slot_rank = jnp.sum((same_owner & earlier).astype(jnp.int32), axis=1)
    slot_index = owners * capacity + slot_rank
    row_weight = jnp.repeat(exposure_weight.astype(jnp.bfloat16), blocks_each)
    weight_cols = jnp.where(
        columns[:, None] == jnp.arange(PW)[None, :],
        row_weight[:, None],
        jnp.zeros((), jnp.bfloat16),
    )
    send_blocks = (
        jnp.zeros((devices * capacity, BLOCK, BLOCK), jnp.bfloat16)
        .at[slot_index]
        .set(shifted.astype(jnp.bfloat16))
    )
    send_weights = jnp.zeros((devices * capacity, PW), jnp.bfloat16).at[slot_index].set(weight_cols)
    got_blocks, got_weights = (
        lax.all_to_all(
            send_blocks.reshape(devices, capacity, BLOCK, BLOCK),
            ("visit", "sky"),
            split_axis=0,
            concat_axis=0,
            tiled=True,
        ),
        lax.all_to_all(
            send_weights.reshape(devices, capacity, PW),
            ("visit", "sky"),
            split_axis=0,
            concat_axis=0,
            tiled=True,
        ),
    )
    got_blocks = got_blocks.reshape(devices * capacity, BLOCK, BLOCK)
    got_weights = got_weights.reshape(devices * capacity, PW)
    summed = jnp.einsum("sj,sab->jab", got_weights, got_blocks, preferred_element_type=jnp.float32)
    total_weight = jnp.sum(got_weights.astype(jnp.float32), axis=0)
    coadd = summed / (1.0 + total_weight)[:, None, None]
    strip = coadd.transpose(1, 0, 2).reshape(BLOCK, PW * BLOCK)
    levels = threshold_level.astype(jnp.float32)
    first_row = lax.axis_index(("visit", "sky")) * BLOCK
    sky_rows = devices * BLOCK
    wide = extended(strip, ((("visit", "sky"), 0),), SWEEPS * reach_rows)
    for sweep_number in range(SWEEPS):
        wide = sweep(wide, first_row - (SWEEPS - sweep_number) * reach_rows, levels, sky_rows)
    strip = wide
    template_bf = strip.astype(jnp.bfloat16).reshape(BLOCK, PW, BLOCK).transpose(1, 0, 2)
    live_cols = (got_weights > 0).astype(jnp.bfloat16)
    answers = jnp.einsum(
        "sj,jab->sab", live_cols, template_bf, preferred_element_type=jnp.float32
    ).astype(jnp.bfloat16)
    returned = lax.all_to_all(
        answers.reshape(devices, capacity, BLOCK, BLOCK),
        ("visit", "sky"),
        split_axis=0,
        concat_axis=0,
        tiled=True,
    )
    returned = returned.reshape(devices * capacity, BLOCK, BLOCK)[slot_index]
    difference = shifted - returned.astype(jnp.float32)
    difference = (
        difference.reshape(exposures_here, tile_count, tile_count, BLOCK, BLOCK)
        .transpose(0, 1, 3, 2, 4)
        .reshape(exposures_here, cut_side, cut_side)
    )
    return (strip, difference)


def solution(mesh):
    placed = (
        P(("visit", "sky"), None, None),
        P(("visit", "sky"), None, None),
        P(("visit", "sky"), None, None),
        P(("visit", "sky"), None, None),
        P(("visit", "sky")),
        P(("visit", "sky"), None, None),
        P(("visit", "sky"), None),
        P(("visit", "sky"), None),
        P(),
    )
    return jax.shard_map(
        shards,
        mesh=mesh,
        in_specs=placed,
        out_specs=(P(("visit", "sky"), None), P(("visit", "sky"), None, None)),
        check_vma=False,
    )
```

profile of v0, /device:TPU:0, one launch (start us, length us, event | category | flops | bytes accessed | tf_op | source)
XLA Modules:
  0.0 379.0 jit_solution(17411421557699384782)
XLA Ops:
  5.8 7.4 %all-to-all-start = ((bf16[32,2,4]{2,1,0:T(2,128)(2,1)}), bf16[32,2,4]{2,1,0:T(2,128)(2,1)}, u32[]{:S(2)}, u32[]{:S(2)}) async-start(bf16[32,2,4]{2,1,0:T(2,128)(2,1)} %bitcast.16), calls=%async_computation | async-start | bytes 32768 | tf_op jit(solution)/shard_map/all_to_all | solution.py:194
  15.0 221.3 %while.37 = (s32[]{:T(128)}, f32[2,16,128,128]{3,2,1,0:T(8,128)}, s32[2,16]{1,0:T(2,128)S(1)}, bf16[2,512,512]{2,1,0:T(8,128)(2,1)S(1)}, bf16[2,16,21]{2,1,0:T(8...) while((s32[]{:T(128)}, f32[2,16,128,128]{3,2,1,0:T(8,128)}, ...), condition=%wide.region_5.6_spmd, body=%wide.region_2.5_spmd.sunk | while | flops 750921280 | bytes 80118424 | solution.py:166
  18.3 95.6 %while.38 = (s32[]{:T(128)}, f32[4,128,512]{2,1,0:T(8,128)}, s32[4]{0:T(128)S(1)}, bf16[4,532,148]{2,1,0:T(8,128)(2,1)S(1)}, bf16[16,148,128]{2,1,0:T(8,128)(2,1...) while((s32[]{:T(128)}, f32[4,128,512]{2,1,0:T(8,128)}, ...), condition=%wide.region_4.4_spmd.clone.clone, body=%wide.region_3.3_spmd.clone.clone.sunk | while | flops 721259136 | bytes 42367972 | solution.py:76
  31.0 5.5 %copy.140 = f32[16,128,512]{2,0,1:T(8,128)} copy(f32[16,128,512]{1,2,0:T(8,128)} %convolution_bitcast_fusion.2) | data formatting | bytes 8388608 | tf_op jit(solution)/shard_map/while/body/eval_jaxpr/while/body/eval_jaxpr/knm,kmc->knc/dot_general | solution.py:63
  36.5 4.5 %fusion.160 = f32[128,512,4]{1,2,0:T(4,128)S(1)} fusion(f32[16,128,512]{2,0,1:T(8,128)} %copy.140, f32[4,16]{1,0:T(4,128)S(1)} %get-tuple-element.533), kind=kOutput, calls=%fused_computation.17.clone.1 | convolution fusion | flops 50331648 | bytes 5243136 | tf_op jit(solution)/shard_map/while/body/eval_jaxpr/while/body/eval_jaxpr/jk,knc->jnc/dot_general | solution.py:64
  54.9 5.5 %copy.140 = f32[16,128,512]{2,0,1:T(8,128)} copy(f32[16,128,512]{1,2,0:T(8,128)} %convolution_bitcast_fusion.2) | data formatting | bytes 8388608 | tf_op jit(solution)/shard_map/while/body/eval_jaxpr/while/body/eval_jaxpr/knm,kmc->knc/dot_general | solution.py:63
  60.4 4.5 %fusion.160 = f32[128,512,4]{1,2,0:T(4,128)S(1)} fusion(f32[16,128,512]{2,0,1:T(8,128)} %copy.140, f32[4,16]{1,0:T(4,128)S(1)} %get-tuple-element.533), kind=kOutput, calls=%fused_computation.17.clone.1 | convolution fusion | flops 50331648 | bytes 5243136 | tf_op jit(solution)/shard_map/while/body/eval_jaxpr/while/body/eval_jaxpr/jk,knc->jnc/dot_general | solution.py:64
  78.8 5.5 %copy.140 = f32[16,128,512]{2,0,1:T(8,128)} copy(f32[16,128,512]{1,2,0:T(8,128)} %convolution_bitcast_fusion.2) | data formatting | bytes 8388608 | tf_op jit(solution)/shard_map/while/body/eval_jaxpr/while/body/eval_jaxpr/knm,kmc->knc/dot_general | solution.py:63
  84.3 4.5 %fusion.160 = f32[128,512,4]{1,2,0:T(4,128)S(1)} fusion(f32[16,128,512]{2,0,1:T(8,128)} %copy.140, f32[4,16]{1,0:T(4,128)S(1)} %get-tuple-element.533), kind=kOutput, calls=%fused_computation.17.clone.1 | convolution fusion | flops 50331648 | bytes 5243136 | tf_op jit(solution)/shard_map/while/body/eval_jaxpr/while/body/eval_jaxpr/jk,knc->jnc/dot_general | solution.py:64
  102.7 5.5 %copy.140 = f32[16,128,512]{2,0,1:T(8,128)} copy(f32[16,128,512]{1,2,0:T(8,128)} %convolution_bitcast_fusion.2) | data formatting | bytes 8388608 | tf_op jit(solution)/shard_map/while/body/eval_jaxpr/while/body/eval_jaxpr/knm,kmc->knc/dot_general | solution.py:63
  108.2 4.5 %fusion.160 = f32[128,512,4]{1,2,0:T(4,128)S(1)} fusion(f32[16,128,512]{2,0,1:T(8,128)} %copy.140, f32[4,16]{1,0:T(4,128)S(1)} %get-tuple-element.533), kind=kOutput, calls=%fused_computation.17.clone.1 | convolution fusion | flops 50331648 | bytes 5243136 | tf_op jit(solution)/shard_map/while/body/eval_jaxpr/while/body/eval_jaxpr/jk,knc->jnc/dot_general | solution.py:64
  128.9 95.6 %while.38 = (s32[]{:T(128)}, f32[4,128,512]{2,1,0:T(8,128)}, s32[4]{0:T(128)S(1)}, bf16[4,532,148]{2,1,0:T(8,128)(2,1)S(1)}, bf16[16,148,128]{2,1,0:T(8,128)(2,1...) while((s32[]{:T(128)}, f32[4,128,512]{2,1,0:T(8,128)}, ...), condition=%wide.region_4.4_spmd.clone.clone, body=%wide.region_3.3_spmd.clone.clone.sunk | while | flops 721259136 | bytes 42367972 | solution.py:76
  141.6 5.5 %copy.140 = f32[16,128,512]{2,0,1:T(8,128)} copy(f32[16,128,512]{1,2,0:T(8,128)} %convolution_bitcast_fusion.2) | data formatting | bytes 8388608 | tf_op jit(solution)/shard_map/while/body/eval_jaxpr/while/body/eval_jaxpr/knm,kmc->knc/dot_general | solution.py:63
  147.1 4.5 %fusion.160 = f32[128,512,4]{1,2,0:T(4,128)S(1)} fusion(f32[16,128,512]{2,0,1:T(8,128)} %copy.140, f32[4,16]{1,0:T(4,128)S(1)} %get-tuple-element.533), kind=kOutput, calls=%fused_computation.17.clone.1 | convolution fusion | flops 50331648 | bytes 5243136 | tf_op jit(solution)/shard_map/while/body/eval_jaxpr/while/body/eval_jaxpr/jk,knc->jnc/dot_general | solution.py:64
  165.5 5.5 %copy.140 = f32[16,128,512]{2,0,1:T(8,128)} copy(f32[16,128,512]{1,2,0:T(8,128)} %convolution_bitcast_fusion.2) | data formatting | bytes 8388608 | tf_op jit(solution)/shard_map/while/body/eval_jaxpr/while/body/eval_jaxpr/knm,kmc->knc/dot_general | solution.py:63
  171.0 4.5 %fusion.160 = f32[128,512,4]{1,2,0:T(4,128)S(1)} fusion(f32[16,128,512]{2,0,1:T(8,128)} %copy.140, f32[4,16]{1,0:T(4,128)S(1)} %get-tuple-element.533), kind=kOutput, calls=%fused_computation.17.clone.1 | convolution fusion | flops 50331648 | bytes 5243136 | tf_op jit(solution)/shard_map/while/body/eval_jaxpr/while/body/eval_jaxpr/jk,knc->jnc/dot_general | solution.py:64
  189.4 5.5 %copy.140 = f32[16,128,512]{2,0,1:T(8,128)} copy(f32[16,128,512]{1,2,0:T(8,128)} %convolution_bitcast_fusion.2) | data formatting | bytes 8388608 | tf_op jit(solution)/shard_map/while/body/eval_jaxpr/while/body/eval_jaxpr/knm,kmc->knc/dot_general | solution.py:63
  194.9 4.5 %fusion.160 = f32[128,512,4]{1,2,0:T(4,128)S(1)} fusion(f32[16,128,512]{2,0,1:T(8,128)} %copy.140, f32[4,16]{1,0:T(4,128)S(1)} %get-tuple-element.533), kind=kOutput, calls=%fused_computation.17.clone.1 | convolution fusion | flops 50331648 | bytes 5243136 | tf_op jit(solution)/shard_map/while/body/eval_jaxpr/while/body/eval_jaxpr/jk,knc->jnc/dot_general | solution.py:64
  213.3 5.5 %copy.140 = f32[16,128,512]{2,0,1:T(8,128)} copy(f32[16,128,512]{1,2,0:T(8,128)} %convolution_bitcast_fusion.2) | data formatting | bytes 8388608 | tf_op jit(solution)/shard_map/while/body/eval_jaxpr/while/body/eval_jaxpr/knm,kmc->knc/dot_general | solution.py:63
  218.8 4.5 %fusion.160 = f32[128,512,4]{1,2,0:T(4,128)S(1)} fusion(f32[16,128,512]{2,0,1:T(8,128)} %copy.140, f32[4,16]{1,0:T(4,128)S(1)} %get-tuple-element.533), kind=kOutput, calls=%fused_computation.17.clone.1 | convolution fusion | flops 50331648 | bytes 5243136 | tf_op jit(solution)/shard_map/while/body/eval_jaxpr/while/body/eval_jaxpr/jk,knc->jnc/dot_general | solution.py:64
  243.8 5.8 %all-to-all-start.1 = ((bf16[32,2,128,128]{3,1,2,0:T(2,128)(2,1)}), bf16[32,2,128,128]{3,1,2,0:T(2,128)(2,1)S(1)}, u32[]{:S(2)}, u32[]{:S(2)}) async-start(bf16[32,2,128,128]{3,1,2,0:T(2,128)(2,1)} %copy.93), calls=%async_computation.1 | async-start | bytes 4194304 | tf_op jit(solution)/shard_map/all_to_all | solution.py:187
  253.0 45.5 %all-to-all-done.1 = bf16[32,2,128,128]{3,1,2,0:T(2,128)(2,1)S(1)} async-done(((bf16[32,2,128,128]{3,1,2,0:T(2,128)(2,1)}), bf16[32,2,128,128]{3,1,2,0:T(2,128)(2,1)S(1)}, u32[]{:S(2)}, u32[]{:S(2)}) %all-to-all-start.1) | async-done | bytes 2097184 | tf_op jit(solution)/shard_map/all_to_all | solution.py:187
  313.6 7.4 %all-to-all-start.2 = ((bf16[32,2,128,128]{3,1,2,0:T(2,128)(2,1)}), bf16[32,2,128,128]{3,1,2,0:T(2,128)(2,1)S(1)}, u32[]{:S(2)}, u32[]{:S(2)}) async-start(bf16[32,2,128,128]{3,1,2,0:T(2,128)(2,1)} %copy.102), calls=%async_computation.2 | async-start | bytes 4194304 | tf_op jit(solution)/shard_map/all_to_all | solution.py:220
  320.9 48.7 %all-to-all-done.2 = bf16[32,2,128,128]{3,1,2,0:T(2,128)(2,1)S(1)} async-done(((bf16[32,2,128,128]{3,1,2,0:T(2,128)(2,1)}), bf16[32,2,128,128]{3,1,2,0:T(2,128)(2,1)S(1)}, u32[]{:S(2)}, u32[]{:S(2)}) %all-to-all-start.2) | async-done | bytes 2097184 | tf_op jit(solution)/shard_map/all_to_all | solution.py:220
  (247 shorter events, 178.3 us)
Async XLA Ops:
  0.6 14.3 %copy-start.5 = (f32[2,16,21]{2,1,0:T(8,128)S(1)}, f32[2,16,21]{2,1,0:T(8,128)}, u32[]{:S(2)}) copy-start(f32[2,16,21]{2,1,0:T(8,128)} %param.15) | copy-start | bytes 8068
  0.6 14.3 %copy-start.6 = (f32[2,16,21]{2,1,0:T(8,128)S(1)}, f32[2,16,21]{2,1,0:T(8,128)}, u32[]{:S(2)}) copy-start(f32[2,16,21]{2,1,0:T(8,128)} %param.14) | copy-start | bytes 8068
  0.7 14.3 %copy-start.4 = (f32[2,4,16]{2,1,0:T(4,128)S(1)}, f32[2,4,16]{2,1,0:T(4,128)}, u32[]{:S(2)}) copy-start(f32[2,4,16]{2,1,0:T(4,128)} %param.16) | copy-start | bytes 1540
  0.7 14.3 %copy-start.10 = (s32[2,16]{1,0:T(2,128)S(1)}, s32[2,16]{1,0:T(2,128)}, u32[]{:S(2)}) copy-start(s32[2,16]{1,0:T(2,128)} %param.20) | copy-start | bytes 388
  4.5 8.7 %copy-start.7 = (s32[32]{0:T(128)}, s32[32]{0:T(128)S(1)}, u32[]{:S(2)}) copy-start(s32[32]{0:T(128)S(1)} %fusion.121) | copy-start | bytes 388
  5.8 238.0 %all-to-all-start = ((bf16[32,2,4]{2,1,0:T(2,128)(2,1)}), bf16[32,2,4]{2,1,0:T(2,128)(2,1)}, u32[]{:S(2)}, u32[]{:S(2)}) async-start(bf16[32,2,4]{2,1,0:T(2,128)(2,1)} %bitcast.16), calls=%async_computation | async-start | bytes 32768 | tf_op jit(solution)/shard_map/all_to_all | solution.py:194
  18.3 2.0 copy-start
  40.9 1.2 copy-start.1
  42.2 2.0 copy-start
  66.1 2.0 copy-start
  90.0 2.0 copy-start
  112.6 1.2 copy-start.1
  124.3 1.4 copy-start.3
  128.9 2.0 copy-start
  152.8 2.0 copy-start
  176.7 2.0 copy-start
  200.6 2.0 copy-start
  234.9 1.4 copy-start.3
  236.3 2.3 copy-start.8
  243.8 5.9 %copy-start.9 = (s32[32,4]{0,1:T(4,128)S(1)}, s32[32,4]{0,1:T(4,128)}, u32[]{:S(2)}) copy-start(s32[32,4]{0,1:T(4,128)} %param.21) | copy-start | bytes 1540
  243.8 54.7 %all-to-all-start.1 = ((bf16[32,2,128,128]{3,1,2,0:T(2,128)(2,1)}), bf16[32,2,128,128]{3,1,2,0:T(2,128)(2,1)S(1)}, u32[]{:S(2)}, u32[]{:S(2)}) async-start(bf16[32,2,128,128]{3,1,2,0:T(2,128)(2,1)} %copy.93), calls=%async_computation.1 | async-start | bytes 4194304 | tf_op jit(solution)/shard_map/all_to_all | solution.py:187
  299.7 3.2 collective-permute-start
  301.3 4.5 %collective-permute-start.1 = (f32[12,512]{1,0:T(8,128)S(1)}, f32[12,512]{1,0:T(8,128)S(1)}, u32[]{:S(2)}, u32[]{:S(2)}) collective-permute-start(f32[12,512]{1,0:T(8,128)S(1)} %bitcast.184), channel_id=1, source_target_pairs={{1,0},{2,1},{3,2},{4,3},{5,4},{6,5},{7,6},{8,7},{9,8},{10,9},{11,1... | collective-permute-start | bytes 73736 | tf_op jit(solution)/shard_map/ppermute | solution.py:26
  313.6 56.1 %all-to-all-start.2 = ((bf16[32,2,128,128]{3,1,2,0:T(2,128)(2,1)}), bf16[32,2,128,128]{3,1,2,0:T(2,128)(2,1)S(1)}, u32[]{:S(2)}, u32[]{:S(2)}) async-start(bf16[32,2,128,128]{3,1,2,0:T(2,128)(2,1)} %copy.102), calls=%async_computation.2 | async-start | bytes 4194304 | tf_op jit(solution)/shard_map/all_to_all | solution.py:220
  (8 other events, 9.4 us)
where the time goes:
time: 382 us; the launch traced here: 379 us
  local copies, waits for them, and re-layouts  147 us (38%)
  waiting for transfers between devices  97.1 us (25%)
  matrix products  81.8 us (21%)
  other arithmetic  23.6 us (6%)
  starting transfers between devices  23.4 us (6%)
  loops' own time  5.09 us (1%)
    reshape x16, local copies, waits for them, and re-layouts, row_tile(): smeared.astype(jnp.bfloat16).reshape(across.shape[0], window_rows, cut_side)  49.8 us
    all_to_all x1, waiting for transfers between devices, shards(): lax.all_to_all(answers.reshape(devices, capacity, BLOCK, BLOCK), ('visit'...  48.7 us
    all_to_all x1, waiting for transfers between devices, shards(): lax.all_to_all(send_blocks.reshape(devices, capacity, BLOCK, BLOCK), ('vi...  45.5 us
    dot_general x8, local copies, waits for them, and re-layouts, row_tile(): jnp.einsum('knm,kmc->knc', downward, smeared, preferred_element_type=jnp....  44 us
    dot_general x8, matrix products, row_tile(): basis_parts = jnp.einsum('jk,knc->jnc', coeffs, stacked, precision=highest)  35.7 us
    dot_general x8, matrix products, row_tile(): jnp.einsum('knm,kmc->knc', downward, smeared, preferred_element_type=jnp....  35.4 us
    reshape x8, local copies, waits for them, and re-layouts, on_grid(): return raster.reshape(tile_count, BLOCK, tile_count, BLOCK)  9.64 us
  transfers between devices with their start and end apart: 5, of which 3 were waited for; matrix products, arithmetic and copies ran while one was open for 60% of the time, Pallas kernels for 0%

commit v1 on v0

v1 whole, which is shorter than its diff:
```python
import functools
import jax
import jax.numpy as jnp
from jax import lax
from jax.experimental import pallas as pl
from jax.experimental.pallas import tpu as pltpu
from jax.sharding import PartitionSpec as P

BLOCK = 128
PW = 4
SWEEPS = 2
TAIL = 32
TOP = 16

highest = lax.Precision.HIGHEST
spline_taps = (0.0625, 0.25, 0.375, 0.25, 0.0625)
fine_tau = 0.04
coarse_tau = 0.02
reach_rows = 6


def conv_kernel(
    shift_ref,
    owner_ref,
    column_ref,
    weight_ref,
    x_ref,
    across_ref,
    down_ref,
    coef_ref,
    shifted_ref,
    dense_ref,
    padded,
    across,
    band,
    mixing,
    smeared,
    conv,
    conv_right,
):
    exposure = pl.program_id(0)
    side = x_ref.shape[1]
    tiles = side // BLOCK
    kernels = across_ref.shape[1]
    window = BLOCK + TAIL
    wide = side + BLOCK

    @pl.when(exposure == 0)
    def _():
        dense_ref[...] = jnp.zeros_like(dense_ref)

    padded[0:TOP, :] = jnp.zeros((TOP, wide), jnp.bfloat16)
    padded[TOP + side : TOP + side + TOP, :] = jnp.zeros((TOP, wide), jnp.bfloat16)
    for t in range(tiles):
        rows = jnp.concatenate(
            [x_ref[0, t * BLOCK : (t + 1) * BLOCK, :], jnp.zeros((BLOCK, BLOCK), jnp.float32)],
            axis=1,
        )
        padded[TOP + t * BLOCK : TOP + (t + 1) * BLOCK, :] = pltpu.roll(rows, 10, 1).astype(
            jnp.bfloat16
        )

    for k in range(kernels):
        line = jnp.broadcast_to(across_ref[0, k : k + 1, :], (2 * BLOCK, 2 * BLOCK))
        line = pltpu.roll(line, 0, 1, stride=1, stride_axis=0)
        across[:, k * BLOCK : (k + 1) * BLOCK] = line[:, :BLOCK].astype(jnp.bfloat16)
    per = BLOCK // TAIL
    for g in range(kernels // per):
        tail = None
        for q in range(per):
            k = g * per + q
            line = jnp.broadcast_to(down_ref[0, k : k + 1, :], (BLOCK, 2 * BLOCK))
            line = pltpu.roll(line, 0, 1, stride=1, stride_axis=0)
            band[:, k * BLOCK : (k + 1) * BLOCK] = line[:, :BLOCK]
            part = line[:, BLOCK:]
            if q:
                part = pltpu.roll(part, q * TAIL, 1)
            tail = part if tail is None else tail + part
        first = kernels * BLOCK + g * BLOCK
        band[:, first : first + BLOCK] = tail

    lane = lax.broadcasted_iota(jnp.int32, (1, side), 1).astype(jnp.float32)
    v = (lane + 0.5) / side - 0.5

    def row_tile(t, carry):
        first = pl.multiple_of(t * BLOCK, BLOCK)
        stacked = jnp.concatenate(
            [
                padded[pl.ds(first, window), c * BLOCK : (c + 2) * BLOCK]
                for c in range(tiles)
            ],
            axis=0,
        )
        for pair in range(kernels // 2):
            out = jnp.dot(
                stacked,
                across[:, pair * 2 * BLOCK : (pair + 1) * 2 * BLOCK],
                preferred_element_type=jnp.float32,
            ).astype(jnp.bfloat16)
            for half in range(2):
                k = 2 * pair + half
                for c in range(tiles):
                    piece = out[
                        c * window : (c + 1) * window, half * BLOCK : (half + 1) * BLOCK
                    ]
                    lanes = slice(c * BLOCK, (c + 1) * BLOCK)
                    smeared[k * BLOCK : (k + 1) * BLOCK, lanes] = piece[:BLOCK]
                    low = kernels * BLOCK + k * TAIL
                    smeared[low : low + TAIL, lanes] = piece[BLOCK:]
        row = (first + lax.broadcasted_iota(jnp.int32, (BLOCK, 1), 0)).astype(jnp.float32)
        u = (row + 0.5) / side - 0.5
        depth = band.shape[1]
        step = 4 * BLOCK
        for j in range(depth // step):
            s = slice(j * step, (j + 1) * step)
            b = band[:, s]
            c = coef_ref[0, :, s]
            mixing[:BLOCK, s] = ((c[0:1] + u * c[1:2]) * b).astype(jnp.bfloat16)
            mixing[BLOCK:, s] = ((c[2:3] + u * c[3:4]) * b).astype(jnp.bfloat16)
        total = jnp.dot(mixing[...], smeared[...], preferred_element_type=jnp.float32)
        value = total[:BLOCK] + v * total[BLOCK:]
        conv[pl.ds(first, BLOCK), :] = value
        moved = pltpu.roll(value, side - 1, 1)
        conv_right[pl.ds(first, BLOCK), :] = jnp.where(
            lax.broadcasted_iota(jnp.int32, (1, side), 1) < side - 1, moved, 0.0
        )
        return carry

    lax.fori_loop(0, tiles, row_tile, 0)
    conv[side : side + 8, :] = jnp.zeros((8, side), jnp.float32)
    conv_right[side : side + 8, :] = jnp.zeros((8, side), jnp.float32)

    def quarter(number):
        return (number.astype(jnp.float32) + 0.5) / 4.0

    weight = weight_ref[exposure]
    for p in range(tiles):
        for q in range(tiles):
            b = p * tiles + q
            s = shift_ref[exposure, b]
            fx = quarter(lax.rem(s, 4))
            fy = quarter(lax.div(s, 4))
            r = slice(p * BLOCK, (p + 1) * BLOCK)
            below = slice(p * BLOCK + 1, (p + 1) * BLOCK + 1)
            lanes = slice(q * BLOCK, (q + 1) * BLOCK)
            value = (1.0 - fy) * ((1.0 - fx) * conv[r, lanes] + fx * conv_right[r, lanes]) + fy * (
                (1.0 - fx) * conv[below, lanes] + fx * conv_right[below, lanes]
            )
            shifted_ref[0, r, lanes] = value
            sent = weight * value.astype(jnp.bfloat16).astype(jnp.float32)
            at = (
                pl.ds(pl.multiple_of(owner_ref[exposure, b] * BLOCK, BLOCK), BLOCK),
                pl.ds(pl.multiple_of(column_ref[exposure, b] * BLOCK, BLOCK), BLOCK),
            )
            dense_ref[at] = (dense_ref[at].astype(jnp.float32) + sent).astype(jnp.bfloat16)


def difference_kernel(owner_ref, column_ref, shifted_ref, sky_ref, out_ref):
    exposure, p = pl.program_id(0), pl.program_id(1)
    tiles = shifted_ref.shape[2] // BLOCK
    for q in range(tiles):
        b = p * tiles + q
        at = (
            pl.ds(pl.multiple_of(owner_ref[exposure, b] * BLOCK, BLOCK), BLOCK),
            pl.ds(pl.multiple_of(column_ref[exposure, b] * BLOCK, BLOCK), BLOCK),
        )
        lanes = slice(q * BLOCK, (q + 1) * BLOCK)
        out_ref[0, :, lanes] = shifted_ref[0, :, lanes] - sky_ref[at].astype(jnp.float32)


def extended(shard, sides, width):
    for axis, dim in sides:
        peers, length = (lax.axis_size(axis), shard.shape[dim])
        up = [(i, (i + 1) % peers) for i in range(peers - 1)]
        down = [(j, i) for i, j in up]
        last = lax.slice_in_dim(shard, length - width, length, axis=dim)
        leading = lax.slice_in_dim(shard, 0, width, axis=dim)
        before = lax.ppermute(last, axis, up)
        after = lax.ppermute(leading, axis, down)
        shard = jnp.concatenate([before, shard, after], axis=dim)
    return shard


def smooth_rows(raster, dilation):
    kept_rows = raster.shape[0] - 4 * dilation
    summed = spline_taps[0] * raster[0:kept_rows]
    for offset in range(1, 5):
        summed = (
            summed + spline_taps[offset] * raster[offset * dilation : offset * dilation + kept_rows]
        )
    return summed


def smooth_cols(raster, dilation):
    col_count = raster.shape[1]
    padded = jnp.pad(raster, ((0, 0), (2 * dilation, 2 * dilation)))
    summed = spline_taps[0] * padded[:, 0:col_count]
    for offset in range(1, 5):
        summed = (
            summed
            + spline_taps[offset] * padded[:, offset * dilation : offset * dilation + col_count]
        )
    return summed


def shrink(detail, limit):
    return detail - jnp.clip(detail, -limit, limit)


def level_map(first_row, row_count, levels):
    owner_rows = jnp.clip((first_row + jnp.arange(row_count)) // BLOCK, 0, levels.shape[0] - 1)
    one_hot = (owner_rows[:, None] == jnp.arange(levels.shape[0])[None, :]).astype(jnp.float32)
    per_row = jnp.dot(one_hot, levels, precision=highest)
    return jnp.repeat(per_row, BLOCK, axis=1)


def sweep(wide, first_row, levels, sky_rows):
    row_count = wide.shape[0]
    positions = first_row + jnp.arange(row_count)
    inside = ((positions >= 0) & (positions < sky_rows)).astype(jnp.float32)[:, None]
    coarse_zero = wide * inside
    coarse_one = smooth_cols(smooth_rows(coarse_zero, 1), 1) * inside[2 : row_count - 2]
    coarse_two = smooth_cols(smooth_rows(coarse_one, 2), 2)
    kept_rows = row_count - 12
    detail_fine = coarse_zero[6 : 6 + kept_rows] - coarse_one[4 : 4 + kept_rows]
    detail_coarse = coarse_one[4 : 4 + kept_rows] - coarse_two
    limits = level_map(first_row + 6, kept_rows, levels)
    return (
        coarse_two
        + shrink(detail_fine, fine_tau * limits)
        + shrink(detail_coarse, coarse_tau * limits)
    )


def bf_values(array):
    return array.astype(jnp.bfloat16).astype(jnp.float32)


def shards(
    cutouts,
    vert_taps,
    horiz_taps,
    field_coeffs,
    exposure_weight,
    dest_owner,
    dest_column,
    shift_index,
    threshold_level,
):
    exposures, side, _ = cutouts.shape
    tiles = side // BLOCK
    kernels, taps = vert_taps.shape[1:]
    axes = ("visit", "sky")
    devices = lax.axis_size("visit") * lax.axis_size("sky")
    sky_rows = devices * BLOCK
    sky_cols = PW * BLOCK
    owners = dest_owner.reshape(exposures, tiles * tiles)
    weight = bf_values(exposure_weight)

    targets = owners * PW + dest_column
    hits = (targets[:, :, None] == jnp.arange(devices * PW)[None, None, :]).astype(jnp.float32)
    own_weights = jnp.sum(hits * weight[:, None, None], axis=(0, 1))
    all_weights = lax.all_gather(own_weights, axes)
    me = lax.axis_index(axes)
    total_weight = lax.dynamic_slice_in_dim(jnp.sum(all_weights, axis=0), me * PW, PW)

    horizontal, vertical = bf_values(horiz_taps), bf_values(vert_taps)
    gap = 2 * BLOCK - taps
    across_rows = jnp.concatenate(
        [
            horizontal[:, :, :1],
            jnp.zeros((exposures, kernels, gap), jnp.float32),
            horizontal[:, :, :0:-1],
        ],
        axis=2,
    )
    margin = (taps - 1) // 2
    down_rows = jnp.pad(
        vertical, ((0, 0), (0, 0), (TOP - margin, gap - (TOP - margin)))
    )
    coef_lanes = jnp.concatenate(
        [jnp.repeat(field_coeffs, BLOCK, axis=2), jnp.repeat(field_coeffs, TAIL, axis=2)], axis=2
    )
    depth = kernels * (BLOCK + TAIL)
    shifted, dense = pl.pallas_call(
        conv_kernel,
        grid_spec=pltpu.PrefetchScalarGridSpec(
            num_scalar_prefetch=4,
            grid=(exposures,),
            in_specs=[
                pl.BlockSpec((1, side, side), lambda e, *_: (e, 0, 0)),
                pl.BlockSpec((1, kernels, 2 * BLOCK), lambda e, *_: (e, 0, 0)),
                pl.BlockSpec((1, kernels, 2 * BLOCK), lambda e, *_: (e, 0, 0)),
                pl.BlockSpec((1, 4, depth), lambda e, *_: (e, 0, 0)),
            ],
            out_specs=[
                pl.BlockSpec((1, side, side), lambda e, *_: (e, 0, 0)),
                pl.BlockSpec((sky_rows, sky_cols), lambda e, *_: (0, 0)),
            ],
            scratch_shapes=[
                pltpu.VMEM((side + 2 * TOP, side + BLOCK), jnp.bfloat16),
                pltpu.VMEM((2 * BLOCK, kernels * BLOCK), jnp.bfloat16),
                pltpu.VMEM((BLOCK, depth), jnp.float32),
                pltpu.VMEM((2 * BLOCK, depth), jnp.bfloat16),
                pltpu.VMEM((depth, side), jnp.bfloat16),
                pltpu.VMEM((side + 8, side), jnp.float32),
                pltpu.VMEM((side + 8, side), jnp.float32),
            ],
        ),
        out_shape=[
            jax.ShapeDtypeStruct((exposures, side, side), jnp.float32),
            jax.ShapeDtypeStruct((sky_rows, sky_cols), jnp.bfloat16),
        ],
        compiler_params=pltpu.CompilerParams(vmem_limit_bytes=56 * 1024 * 1024),
        name="convolve",
    )(shift_index, owners, dest_column, weight, cutouts, across_rows, down_rows, coef_lanes)

    summed = lax.psum_scatter(dense, axes, scatter_dimension=0, tiled=True)
    scale = jnp.repeat(1.0 + total_weight, BLOCK)[None, :]
    strip = summed.astype(jnp.float32) / scale
    levels = threshold_level.astype(jnp.float32)
    first_row = me * BLOCK
    wide = extended(strip, ((axes, 0),), SWEEPS * reach_rows)
    for sweep_number in range(SWEEPS):
        wide = sweep(wide, first_row - (SWEEPS - sweep_number) * reach_rows, levels, sky_rows)
    strip = wide
    sky = lax.all_gather(strip.astype(jnp.bfloat16), axes, axis=0, tiled=True)

    difference = pl.pallas_call(
        difference_kernel,
        grid_spec=pltpu.PrefetchScalarGridSpec(
            num_scalar_prefetch=2,
            grid=(exposures, tiles),
            in_specs=[
                pl.BlockSpec((1, BLOCK, side), lambda e, p, *_: (e, p, 0)),
                pl.BlockSpec((sky_rows, sky_cols), lambda e, p, *_: (0, 0)),
            ],
            out_specs=pl.BlockSpec((1, BLOCK, side), lambda e, p, *_: (e, p, 0)),
        ),
        out_shape=jax.ShapeDtypeStruct((exposures, side, side), jnp.float32),
        compiler_params=pltpu.CompilerParams(vmem_limit_bytes=56 * 1024 * 1024),
        name="difference",
    )(owners, dest_column, shifted, sky)
    return (strip, difference)


def solution(mesh):
    placed = (
        P(("visit", "sky"), None, None),
        P(("visit", "sky"), None, None),
        P(("visit", "sky"), None, None),
        P(("visit", "sky"), None, None),
        P(("visit", "sky")),
        P(("visit", "sky"), None, None),
        P(("visit", "sky"), None),
        P(("visit", "sky"), None),
        P(),
    )
    return jax.shard_map(
        shards,
        mesh=mesh,
        in_specs=placed,
        out_specs=(P(("visit", "sky"), None), P(("visit", "sky"), None, None)),
        check_vma=False,
    )
```

time: 382 us -> 264 us (0.69)
  local copies, waits for them, and re-layouts: 147 us -> 4.09 us
  matrix products: 81.8 us -> 0.45 us
  waiting for transfers between devices: 97.1 us -> 160 us
  blocking collectives: 0 us -> 43.1 us
  Pallas kernels: 0 us -> 30.1 us
  starting transfers between devices: 23.4 us -> 2.66 us
  other arithmetic: 23.6 us -> 8.88 us
  between operations: 1.06 us -> 14.3 us
  loops' own time: 5.09 us -> 0 us
    reduce_scatter x0 -> x1, waiting for transfers between devices: none -> 99.1 us  [shards(): summed = lax.psum_scatter(dense, axes, scatter_dimension=0, tiled=True)]
    all_to_all x3 -> x0, waiting for transfers between devices: 94.2 us -> none  [the longest x1 48.7 us: shards(): lax.all_to_all(answers.reshape(devices, capacity, BLOCK, BLOCK), ('visit'...]
    dot_general x30 -> x0, matrix products: 81.4 us -> none  [the longest x8 35.7 us: row_tile(): basis_parts = jnp.einsum('jk,knc->jnc', coeffs, stacked, precision=highest)]
    reshape x28 -> x2, local copies, waits for them, and re-layouts: 68.4 us -> 0.13 us  [the longest x1 0.1 us: shards(): jnp.repeat(field_coeffs, TAIL, axis=2)]
    all_gather x0 -> x1, waiting for transfers between devices: none -> 60.6 us  [shards(): sky = lax.all_gather(strip.astype(jnp.bfloat16), axes, axis=0, tiled=True)]
    dot_general x16 -> x0, local copies, waits for them, and re-layouts: 46.7 us -> none  [the longest x8 44 us: row_tile(): jnp.einsum('knm,kmc->knc', downward, smeared, preferred_element_type=jnp....]
    all_gather x0 -> x1, blocking collectives: none -> 43.1 us  [shards(): all_weights = lax.all_gather(own_weights, axes)]
    pallas_call x0 -> x2, Pallas kernels: none -> 30.1 us  [the longest x1 22.3 us: shards(): pl.pallas_call(conv_kernel, grid_spec=pltpu.PrefetchScalarGridSpec(num_sc...]
  transfers between devices with their start and end apart: 5 -> 4, of which waited for: 3 -> 3; matrix products, arithmetic and copies ran while one was open for 60% -> 1% of each run, Pallas kernels for 0% -> 0%
where the time goes in v1:
time: 264 us
  waiting for transfers between devices  160 us (61%)
  blocking collectives  43.1 us (16%)
  Pallas kernels  30.1 us (11%)
  between operations  14.3 us (5%)
  other arithmetic  8.88 us (3%)
  local copies, waits for them, and re-layouts  4.09 us (2%)
  starting transfers between devices  2.66 us (1%)
    reduce_scatter x1, waiting for transfers between devices, shards(): summed = lax.psum_scatter(dense, axes, scatter_dimension=0, tiled=True)  99.1 us
    all_gather x1, waiting for transfers between devices, shards(): sky = lax.all_gather(strip.astype(jnp.bfloat16), axes, axis=0, tiled=True)  60.6 us
    all_gather x1, blocking collectives, shards(): all_weights = lax.all_gather(own_weights, axes)  43.1 us
    pallas_call x1, Pallas kernels, shards(): pl.pallas_call(conv_kernel, grid_spec=pltpu.PrefetchScalarGridSpec(num_sc...  22.3 us
    pallas_call x1, Pallas kernels, shards(): pl.pallas_call(difference_kernel, grid_spec=pltpu.PrefetchScalarGridSpec(...  7.8 us
  transfers between devices with their start and end apart: 4, of which 3 were waited for; matrix products, arithmetic and copies ran while one was open for 1% of the time, Pallas kernels for 0%

profile of v1, /device:TPU:0, one launch (start us, length us, event | category | flops | bytes accessed | tf_op | source)
XLA Modules:
  0.0 263.9 jit_solution(6745638850212357831)
XLA Ops:
  7.2 1.2 convert_convert_fusion.1.weight_ref
  8.4 0.7 convert_element_type.56
  9.2 0.7 convert_convert_fusion
  10.0 0.7 pad_convert_fusion.down_ref
  10.7 0.8 broadcast_in_dim.33
  11.6 0.8 broadcast_in_dim.32
  12.5 0.7 pad_maximum_fusion.coef_ref
  13.1 0.7 pad_maximum_fusion.1.across_ref
  13.8 22.3 %convolve.1 = (f32[2,512,512]{2,1,0:T(8,128)}, bf16[4096,512]{1,0:T(8,128)(2,1)}) custom-call(s32[2,16]{1,0:T(2,128)} %shift_ref.1, s32[2,16]{1,0:T(2,128)} %bitcast.50, s32[2,16]{1,0:T(2,128)} %column_ref.3, f32[2]{0:T(128)} %convert_convert_fusion.1.weight_ref, f32[2,512,512]{2,1,0:T(8,128)} %x_ref.1, f32[2,16,256]{2,1,0:T(8,128)} %pad_maximum_fusion.1.across_ref, ...), custom_call_target="tpu_custom_call" | custom-call | tf_op jit(solution)/shard_map/convolve/pallas_call | solution.py:285
  36.3 0.6 copy-done
  36.9 43.1 %all-gather.1 = f32[32,1,128]{2,1,0:T(1,128)S(1)} all-gather(f32[1,1,128]{2,1,0:T(1,128)S(1)} %bitcast.53), channel_id=2, replica_groups=mesh['visit'=4,'sky'=8] {'visit','sky'}, dimensions={0}, use_global_device_ids=true | all-gather | bytes 16896 | tf_op jit(solution)/shard_map/all_gather | solution.py:263
  80.5 0.3 broadcast_multiply_fusion.1
  80.7 99.1 %reduce-scatter.2.cloned.1.call-done = bf16[128,512]{1,0:T(8,128)(2,1)} async-done(((bf16[4096,512]{1,0:T(8,128)(2,1)}), bf16[128,512]{1,0:T(8,128)(2,1)}) %reduce-scatter.2.cloned.1.call-update) | async-done | bytes 131088 | tf_op jit(solution)/shard_map/reduce_scatter | solution.py:318
  179.8 0.9 convert_divide_fusion
  180.8 1.3 collective-permute-start
  182.1 1.3 collective-permute-start.1
  184.0 0.2 broadcast_in_dim.36
  184.6 0.6 collective-permute-done.1
  185.5 0.4 fusion.5
  186.0 0.4 add_multiply_fusion
  186.6 0.4 fusion.30
  187.5 1.1 fusion.64
  188.6 60.6 %all-gather.4.cloned.1.call-done.sky_ref = bf16[4096,512]{1,0:T(8,128)(2,1)} async-done(((bf16[128,512]{1,0:T(8,128)(2,1)}), bf16[4096,512]{1,0:T(8,128)(2,1)}) %all-gather.4.cloned.1.call-update) | async-done | bytes 4194320 | tf_op jit(solution)/shard_map/all_gather | solution.py:327
  249.3 7.8 %difference.1 = f32[2,512,512]{2,1,0:T(8,128)} custom-call(s32[2,16]{1,0:T(2,128)} %bitcast.51, s32[2,16]{1,0:T(2,128)} %column_ref.3, f32[2,512,512]{2,1,0:T(8,128)} %get-tuple-element.5.shifted_ref, bf16[4096,512]{1,0:T(8,128)(2,1)} %all-gather.4.cloned.1.call-done.sky_ref), custom_call_target="tpu_custom_call" | custom-call | tf_op jit(solution)/shard_map/difference/pallas_call | solution.py:329
  (47 shorter events, 3.1 us)
Async XLA Ops:
  7.2 172.7 %reduce-scatter.2.cloned.1.call-start = ((), (), s32[]{:S(2)}) async-start(), calls=%async_computation.1 | async-start | bytes 4325376 | tf_op jit(solution)/shard_map/reduce_scatter | solution.py:318
  36.1 0.7 copy-start
  36.1 0.7 copy-start.1
  36.2 0.7 copy-start.2
  36.2 44.1 %copy-start.3 = (s32[32,4]{0,1:T(4,128)S(1)}, s32[32,4]{0,1:T(4,128)}, u32[]{:S(2)}) copy-start(s32[32,4]{0,1:T(4,128)} %param.17) | copy-start | bytes 1540
  36.2 213.1 %all-gather.4.cloned.1.call-start = ((), (), s32[]{:S(2)}) async-start(), calls=%async_computation.2 | async-start | bytes 4325376 | tf_op jit(solution)/shard_map/all_gather | solution.py:327
  180.8 3.8 %collective-permute-start = (f32[12,512]{1,0:T(8,128)S(1)}, f32[12,512]{1,0:T(8,128)S(1)}, u32[]{:S(2)}, u32[]{:S(2)}) collective-permute-start(f32[12,512]{1,0:T(8,128)S(1)} %get-tuple-element.8), channel_id=1, source_target_pairs={{0,1},{1,2},{2,3},{3,4},{4,5},{5,6},{6,7},{7,8},{8,9},{9,10},{10,1... | collective-permute-start | bytes 73736 | tf_op jit(solution)/shard_map/ppermute | solution.py:178
  182.1 3.1 %collective-permute-start.1 = (f32[12,512]{1,0:T(8,128)S(1)}, f32[12,512]{1,0:T(8,128)S(1)}, u32[]{:S(2)}, u32[]{:S(2)}) collective-permute-start(f32[12,512]{1,0:T(8,128)S(1)} %get-tuple-element.9), channel_id=1, source_target_pairs={{1,0},{2,1},{3,2},{4,3},{5,4},{6,5},{7,6},{8,7},{9,8},{10,9},{11,1... | collective-permute-start | bytes 73736 | tf_op jit(solution)/shard_map/ppermute | solution.py:179
Sparse Core Ops, SparseCore 0:
  36.3 143.4 reduce-scatter.1
  188.8 60.4 all-gather.3

commit v2 on v1

v2 whole, which is shorter than its diff:
```python
import functools
import jax
import jax.numpy as jnp
from jax import lax
from jax.experimental import pallas as pl
from jax.experimental.pallas import tpu as pltpu
from jax.sharding import PartitionSpec as P

BLOCK = 128
PW = 4
SWEEPS = 2
TAIL = 32
TOP = 16

spline_taps = (0.0625, 0.25, 0.375, 0.25, 0.0625)
fine_tau = 0.04
coarse_tau = 0.02


def bf_values(array):
    return array.astype(jnp.bfloat16).astype(jnp.float32)


def conv_kernel(
    shift_ref,
    owner_ref,
    column_ref,
    weight_ref,
    factor_ref,
    x_ref,
    across_ref,
    down_ref,
    shifted_ref,
    dense_ref,
    total_ref,
    padded,
    tap_rows,
    coef,
    across,
    band,
    mixing,
    smeared,
    conv,
    conv_right,
):
    exposure = pl.program_id(0)
    side = x_ref.shape[1]
    tiles = side // BLOCK
    kernels = across_ref.shape[1]
    window = BLOCK + TAIL
    wide = side + BLOCK

    @pl.when(exposure == 0)
    def _():
        dense_ref[...] = jnp.zeros_like(dense_ref)
        total_ref[...] = jnp.zeros_like(total_ref)

    padded[0:TOP, :] = jnp.zeros((TOP, wide), jnp.bfloat16)
    padded[TOP + side : TOP + side + TOP, :] = jnp.zeros((TOP, wide), jnp.bfloat16)
    for t in range(tiles):
        rows = jnp.concatenate(
            [x_ref[0, t * BLOCK : (t + 1) * BLOCK, :], jnp.zeros((BLOCK, BLOCK), jnp.float32)],
            axis=1,
        )
        padded[TOP + t * BLOCK : TOP + (t + 1) * BLOCK, :] = pltpu.roll(rows, 10, 1).astype(
            jnp.bfloat16
        )

    taps = across_ref.shape[2]
    margin = (taps - 1) // 2
    source = lax.broadcasted_iota(jnp.int32, (BLOCK, 2 * BLOCK), 0)
    place = lax.broadcasted_iota(jnp.int32, (BLOCK, 2 * BLOCK), 1)
    backward = (place == lax.rem(2 * BLOCK - source, 2 * BLOCK)) & (source < taps)
    forward = (place == source + (TOP - margin)) & (source < taps)

    def lined(taps_ref, at):
        tap_rows[...] = jnp.zeros_like(tap_rows)
        tap_rows[:, :taps] = taps_ref[0]
        return jnp.dot(
            tap_rows[...].astype(jnp.bfloat16),
            at.astype(jnp.float32).astype(jnp.bfloat16),
            preferred_element_type=jnp.float32,
        )

    across_lines = lined(across_ref, backward)
    down_lines = lined(down_ref, forward)
    quarter_of = lax.broadcasted_iota(jnp.int32, (1, BLOCK), 1) // TAIL
    for j in range(4):
        for k in range(kernels):
            coef[j : j + 1, k * BLOCK : (k + 1) * BLOCK] = jnp.full(
                (1, BLOCK), factor_ref[exposure, j, k]
            )
        for g in range(kernels * TAIL // BLOCK):
            row = jnp.zeros((1, BLOCK), jnp.float32)
            for q in range(BLOCK // TAIL):
                row = jnp.where(
                    quarter_of == q, factor_ref[exposure, j, g * (BLOCK // TAIL) + q], row
                )
            low = kernels * BLOCK + g * BLOCK
            coef[j : j + 1, low : low + BLOCK] = row

    for k in range(kernels):
        line = jnp.broadcast_to(across_lines[k : k + 1, :], (2 * BLOCK, 2 * BLOCK))
        line = pltpu.roll(line, 0, 1, stride=1, stride_axis=0)
        across[:, k * BLOCK : (k + 1) * BLOCK] = line[:, :BLOCK].astype(jnp.bfloat16)
    per = BLOCK // TAIL
    for g in range(kernels // per):
        tail = None
        for q in range(per):
            k = g * per + q
            line = jnp.broadcast_to(down_lines[k : k + 1, :], (BLOCK, 2 * BLOCK))
            line = pltpu.roll(line, 0, 1, stride=1, stride_axis=0)
            band[:, k * BLOCK : (k + 1) * BLOCK] = line[:, :BLOCK]
            part = line[:, BLOCK:]
            if q:
                part = pltpu.roll(part, q * TAIL, 1)
            tail = part if tail is None else tail + part
        first = kernels * BLOCK + g * BLOCK
        band[:, first : first + BLOCK] = tail

    lane = lax.broadcasted_iota(jnp.int32, (1, side), 1).astype(jnp.float32)
    v = (lane + 0.5) / side - 0.5

    def row_tile(t, carry):
        first = pl.multiple_of(t * BLOCK, BLOCK)
        stacked = jnp.concatenate(
            [
                padded[pl.ds(first, window), c * BLOCK : (c + 2) * BLOCK]
                for c in range(tiles)
            ],
            axis=0,
        )
        for pair in range(kernels // 2):
            out = jnp.dot(
                stacked,
                across[:, pair * 2 * BLOCK : (pair + 1) * 2 * BLOCK],
                preferred_element_type=jnp.float32,
            ).astype(jnp.bfloat16)
            for half in range(2):
                k = 2 * pair + half
                for c in range(tiles):
                    piece = out[
                        c * window : (c + 1) * window, half * BLOCK : (half + 1) * BLOCK
                    ]
                    lanes = slice(c * BLOCK, (c + 1) * BLOCK)
                    smeared[k * BLOCK : (k + 1) * BLOCK, lanes] = piece[:BLOCK]
                    low = kernels * BLOCK + k * TAIL
                    smeared[low : low + TAIL, lanes] = piece[BLOCK:]
        row = (first + lax.broadcasted_iota(jnp.int32, (BLOCK, 1), 0)).astype(jnp.float32)
        u = (row + 0.5) / side - 0.5
        depth = band.shape[1]
        step = 4 * BLOCK
        for j in range(depth // step):
            s = slice(j * step, (j + 1) * step)
            b = band[:, s]
            c = coef[:, s]
            mixing[:BLOCK, s] = ((c[0:1] + u * c[1:2]) * b).astype(jnp.bfloat16)
            mixing[BLOCK:, s] = ((c[2:3] + u * c[3:4]) * b).astype(jnp.bfloat16)
        total = jnp.dot(mixing[...], smeared[...], preferred_element_type=jnp.float32)
        value = total[:BLOCK] + v * total[BLOCK:]
        conv[pl.ds(first, BLOCK), :] = value
        moved = pltpu.roll(value, side - 1, 1)
        conv_right[pl.ds(first, BLOCK), :] = jnp.where(
            lax.broadcasted_iota(jnp.int32, (1, side), 1) < side - 1, moved, 0.0
        )
        return carry

    lax.fori_loop(0, tiles, row_tile, 0)
    conv[side : side + 8, :] = jnp.zeros((8, side), jnp.float32)
    conv_right[side : side + 8, :] = jnp.zeros((8, side), jnp.float32)

    def quarter(number):
        return (number.astype(jnp.float32) + 0.5) / 4.0

    weight = bf_values(jnp.full((8, BLOCK), weight_ref[exposure]))
    lanes_of = lax.broadcasted_iota(jnp.int32, (8, BLOCK), 1)
    for p in range(tiles):
        for q in range(tiles):
            b = p * tiles + q
            s = shift_ref[exposure, b]
            fx = quarter(lax.rem(s, 4))
            fy = quarter(lax.div(s, 4))
            r = slice(p * BLOCK, (p + 1) * BLOCK)
            below = slice(p * BLOCK + 1, (p + 1) * BLOCK + 1)
            lanes = slice(q * BLOCK, (q + 1) * BLOCK)
            value = (1.0 - fy) * ((1.0 - fx) * conv[r, lanes] + fx * conv_right[r, lanes]) + fy * (
                (1.0 - fx) * conv[below, lanes] + fx * conv_right[below, lanes]
            )
            shifted_ref[0, r, lanes] = value
            sent = weight[0:1] * value.astype(jnp.bfloat16).astype(jnp.float32)
            at = (
                pl.ds(pl.multiple_of(owner_ref[exposure, b] * BLOCK, BLOCK), BLOCK),
                pl.ds(pl.multiple_of(column_ref[exposure, b] * BLOCK, BLOCK), BLOCK),
            )
            owner = owner_ref[exposure, b]
            total_ref[owner] = total_ref[owner] + jnp.where(
                lanes_of == column_ref[exposure, b], weight, 0.0
            )
            dense_ref[at] = (dense_ref[at].astype(jnp.float32) + sent).astype(jnp.bfloat16)


def difference_kernel(owner_ref, column_ref, shifted_ref, sky_ref, out_ref, blocks, sems):
    exposure, p = pl.program_id(0), pl.program_id(1)
    tiles = shifted_ref.shape[2] // BLOCK
    exposures = owner_ref.shape[0]

    def fetch(e, b):
        source = sky_ref.at[
            pl.ds(pl.multiple_of(owner_ref[e, b] * BLOCK, BLOCK), BLOCK),
            pl.ds(pl.multiple_of(column_ref[e, b] * BLOCK, BLOCK), BLOCK),
        ]
        return pltpu.make_async_copy(source, blocks.at[e, b], sems.at[e, b])

    @pl.when((exposure == 0) & (p == 0))
    def _():
        for e in range(exposures):
            for b in range(tiles * tiles):
                fetch(e, b).start()

    for q in range(tiles):
        b = p * tiles + q
        fetch(exposure, b).wait()
        lanes = slice(q * BLOCK, (q + 1) * BLOCK)
        out_ref[0, :, lanes] = shifted_ref[0, :, lanes] - blocks[exposure, b].astype(jnp.float32)


def spline(values, dilation, axis):
    size = values.shape[axis]
    d = dilation
    near = pltpu.roll(values, d, axis) + pltpu.roll(values, size - d, axis)
    far = pltpu.roll(values, 2 * d, axis) + pltpu.roll(values, size - 2 * d, axis)
    return spline_taps[0] * far + spline_taps[1] * near + spline_taps[2] * values


def shrink(detail, limit):
    return detail - jnp.minimum(jnp.maximum(detail, -limit), limit)


def smooth(values, dilation):
    rows, cols = values.shape
    down = spline(values, dilation, 0)
    wide = jnp.concatenate([down, jnp.zeros((rows, BLOCK), jnp.float32)], axis=1)
    return spline(wide, dilation, 1)[:, :cols]


def combine_kernel(
    visits,
    pairs,
    dense_ref,
    weight_ref,
    level_ref,
    strip_ref,
    sky_ref,
    part,
    from_twin,
    from_plane,
    going,
    from_visit,
    w_part,
    w_twin,
    w_plane,
    w_going,
    w_visit,
    edges,
    halo,
    template,
    local_sem,
    twin_sem,
    plane_sem,
    visit_sem,
    w_sem,
    halo_sem,
    back_visit_sem,
    back_plane_sem,
    back_twin_sem,
):
    z = lax.axis_index("visit")
    sky = lax.axis_index("sky")
    peers = 2 * pairs
    devices = visits * peers
    p, core = lax.div(sky, 2), lax.rem(sky, 2)
    me = z * peers + sky
    other = 1 - core

    def linear(number):
        return (lax.div(number, peers), lax.rem(number, peers))

    twin = (z, p * 2 + other)
    places = [lax.rem(p + o, pairs) for o in range(1, pairs)]
    plane = [(z, place * 2 + core) for place in places]
    heights = [lax.rem(z + d, visits) for d in range(1, visits)]
    column = [(height, sky) for height in heights]
    ring = [linear(lax.rem(me + devices - 1, devices)), linear(lax.rem(me + 1, devices))]

    everyone = [twin] + plane + column + ring
    barrier = pltpu.get_barrier_semaphore()
    for peer in everyone:
        pl.semaphore_signal(
            barrier, inc=1, device_id=peer, device_id_type=pl.DeviceIdType.MESH
        )
    pl.semaphore_wait(barrier, len(everyone))

    def send(src, dst, sems, index, peer):
        copy = pltpu.make_async_remote_copy(
            src_ref=src,
            dst_ref=dst,
            send_sem=sems.at[(0,) + index],
            recv_sem=sems.at[(1,) + index],
            device_id=peer,
            device_id_type=pl.DeviceIdType.MESH,
        )
        copy.start()
        sent.append(copy)
        return copy

    sent = []
    order = heights + [z]
    w_copy = send(weight_ref.at[:, :, other], w_twin, w_sem, (0,), twin)
    local, across = [], []
    for j, height in enumerate(order):
        across.append(
            send(dense_ref.at[height, :, other], from_twin.at[j], twin_sem, (j,), twin)
        )
        own = pltpu.make_async_copy(dense_ref.at[height, :, core], part.at[j], local_sem.at[j])
        own.start()
        local.append(own)

    w_copy.wait_recv()
    for height in range(visits):
        for place in range(pairs):
            w_part[place, height] = weight_ref[height, place, core] + w_twin[height, place]
    w_copies = [
        send(w_part.at[place], w_plane.at[o], w_sem, (1 + o,), plane[o])
        for o, place in enumerate(places)
    ]

    def spread(j):
        local[j].wait()
        across[j].wait_recv()

        def add(place, carry):
            part[j, place] = (
                part[j, place].astype(jnp.float32) + from_twin[j, place].astype(jnp.float32)
            ).astype(jnp.bfloat16)
            return carry

        lax.fori_loop(0, pairs, add, 0)
        return [
            send(part.at[j, place], from_plane.at[j, o], plane_sem, (j, o), plane[o])
            for o, place in enumerate(places)
        ]

    def gathered(j):
        total = part[j, p].astype(jnp.float32)
        for o in range(pairs - 1):
            total = total + from_plane[j, o].astype(jnp.float32)
        return total

    moves = [spread(0)]
    for copy in w_copies:
        copy.wait_recv()
    w_total = w_part[p]
    for o in range(pairs - 1):
        w_total = w_total + w_plane[o]
    w_going[...] = w_total
    w_copies = [
        send(w_going.at[height], w_visit.at[j], w_sem, (pairs + j,), column[j])
        for j, height in enumerate(heights)
    ]
    climbs = []
    for j in range(visits):
        if j + 1 < visits:
            moves.append(spread(j + 1))
        for copy in moves[j]:
            copy.wait_recv()
        if j + 1 < visits:
            going[j] = gathered(j).astype(jnp.bfloat16)
            climbs.append(send(going.at[j], from_visit.at[j], visit_sem, (j,), column[j]))
    weight = w_going[z]
    for copy, j in zip(w_copies, range(visits - 1)):
        copy.wait_recv()
        weight = weight + w_visit[j]
    total = gathered(visits - 1)
    for copy, j in zip(climbs, range(visits - 1)):
        copy.wait_recv()
        total = total + from_visit[j].astype(jnp.float32)
    cols = total.shape[1]
    blocks = cols // BLOCK
    scale = jnp.concatenate(
        [jnp.broadcast_to(1.0 + weight[0:1, c : c + 1], (1, BLOCK)) for c in range(blocks)], axis=1
    )
    coadd = total / scale
    edges[0] = coadd[:TOP]
    edges[1] = coadd[BLOCK - TOP :]
    shifts = [
        send(edges.at[0], halo.at[1], halo_sem, (0,), ring[0]),
        send(edges.at[1], halo.at[0], halo_sem, (1,), ring[1]),
    ]
    for copy in shifts:
        copy.wait_recv()

    rows = BLOCK + 2 * TOP
    position = me * BLOCK - TOP + lax.broadcasted_iota(jnp.int32, (rows, 1), 0)
    inside = jnp.where((position >= 0) & (position < devices * BLOCK), 1.0, 0.0)
    above, below = jnp.maximum(me - 1, 0), jnp.minimum(me + 1, devices - 1)

    def levels(owner, height):
        row = level_ref[pl.ds(owner, 1), :].astype(jnp.float32)
        return jnp.concatenate(
            [
                jnp.broadcast_to(row[:, c : c + 1], (height, BLOCK))
                for c in range(blocks)
            ],
            axis=1,
        )

    limits = jnp.concatenate([levels(above, TOP), levels(me, BLOCK), levels(below, TOP)], axis=0)
    values = jnp.concatenate([halo[0], coadd, halo[1]], axis=0)
    for _ in range(SWEEPS):
        values = values * inside
        fine = smooth(values, 1) * inside
        coarse = smooth(fine, 2)
        values = (
            coarse
            + shrink(values - fine, fine_tau * limits)
            + shrink(fine - coarse, coarse_tau * limits)
        )
    strip = values[TOP : TOP + BLOCK]
    strip_ref[...] = strip
    template[...] = strip.astype(jnp.bfloat16)

    mine = sky_ref.at[z, p, core]
    own = pltpu.make_async_copy(template, mine, local_sem.at[visits])
    own.start()
    climbs = [
        send(template, mine, back_visit_sem, (d,), column[d]) for d in range(visits - 1)
    ]
    spreads, twins = [], []

    def outward(d):
        if d == 0:
            source, place = template, mine
        else:
            climbs[d - 1].wait_recv()
            source = place = sky_ref.at[lax.rem(z + visits - d, visits), p, core]
        spreads.append(
            [send(source, place, back_plane_sem, (d, o), plane[o]) for o in range(pairs - 1)]
        )
        twins.append(send(source, place, back_twin_sem, (d, pairs - 1), twin))

    outward(0)
    for d in range(visits):
        if d + 1 < visits:
            outward(d + 1)
        for o in range(pairs - 1):
            spreads[d][o].wait_recv()
            place = sky_ref.at[
                lax.rem(z + visits - d, visits), lax.rem(p + pairs - 1 - o, pairs), core
            ]
            twins.append(send(place, place, back_twin_sem, (d, o), twin))
    for copy in twins:
        copy.wait_recv()
    own.wait()
    for copy in sent:
        copy.wait_send()


def shards(
    cutouts,
    vert_taps,
    horiz_taps,
    field_coeffs,
    exposure_weight,
    dest_owner,
    dest_column,
    shift_index,
    threshold_level,
):
    exposures, side, _ = cutouts.shape
    tiles = side // BLOCK
    kernels, taps = vert_taps.shape[1:]
    axes = ("visit", "sky")
    devices = lax.axis_size("visit") * lax.axis_size("sky")
    sky_rows = devices * BLOCK
    sky_cols = PW * BLOCK
    owners = dest_owner.reshape(exposures, tiles * tiles)

    depth = kernels * (BLOCK + TAIL)
    shifted, dense, weights = pl.pallas_call(
        conv_kernel,
        grid_spec=pltpu.PrefetchScalarGridSpec(
            num_scalar_prefetch=5,
            grid=(exposures,),
            in_specs=[
                pl.BlockSpec((1, side, side), lambda e, *_: (e, 0, 0)),
                pl.BlockSpec((1, kernels, taps), lambda e, *_: (e, 0, 0)),
                pl.BlockSpec((1, kernels, taps), lambda e, *_: (e, 0, 0)),
            ],
            out_specs=[
                pl.BlockSpec((1, side, side), lambda e, *_: (e, 0, 0)),
                pl.BlockSpec((sky_rows, sky_cols), lambda e, *_: (0, 0)),
                pl.BlockSpec((devices, 8, BLOCK), lambda e, *_: (0, 0, 0)),
            ],
            scratch_shapes=[
                pltpu.VMEM((side + 2 * TOP, side + BLOCK), jnp.bfloat16),
                pltpu.VMEM((kernels, BLOCK), jnp.float32),
                pltpu.VMEM((4, depth), jnp.float32),
                pltpu.VMEM((2 * BLOCK, kernels * BLOCK), jnp.bfloat16),
                pltpu.VMEM((BLOCK, depth), jnp.float32),
                pltpu.VMEM((2 * BLOCK, depth), jnp.bfloat16),
                pltpu.VMEM((depth, side), jnp.bfloat16),
                pltpu.VMEM((side + 8, side), jnp.float32),
                pltpu.VMEM((side + 8, side), jnp.float32),
            ],
        ),
        out_shape=[
            jax.ShapeDtypeStruct((exposures, side, side), jnp.float32),
            jax.ShapeDtypeStruct((sky_rows, sky_cols), jnp.bfloat16),
            jax.ShapeDtypeStruct((devices, 8, BLOCK), jnp.float32),
        ],
        compiler_params=pltpu.CompilerParams(vmem_limit_bytes=56 * 1024 * 1024),
        name="convolve",
    )(
        shift_index,
        owners,
        dest_column,
        exposure_weight,
        field_coeffs,
        cutouts,
        horiz_taps,
        vert_taps,
    )

    visits, peers = lax.axis_size("visit"), lax.axis_size("sky")
    pairs = peers // 2
    vmem = pl.BlockSpec(memory_space=pltpu.VMEM)
    piece = (BLOCK, sky_cols)
    tile = (8, BLOCK)

    def sems(*shape):
        return pltpu.SemaphoreType.DMA((2,) + shape)

    strip, sky = pl.pallas_call(
        functools.partial(combine_kernel, visits, pairs),
        in_specs=[
            pl.BlockSpec(memory_space=pl.ANY),
            vmem,
            vmem,
        ],
        out_specs=[vmem, pl.BlockSpec(memory_space=pl.ANY)],
        out_shape=[
            jax.ShapeDtypeStruct(piece, jnp.float32),
            jax.ShapeDtypeStruct((visits, pairs, 2) + piece, jnp.bfloat16),
        ],
        scratch_shapes=[
            pltpu.VMEM((visits, pairs) + piece, jnp.bfloat16),
            pltpu.VMEM((visits, pairs) + piece, jnp.bfloat16),
            pltpu.VMEM((visits, pairs - 1) + piece, jnp.bfloat16),
            pltpu.VMEM((visits - 1,) + piece, jnp.bfloat16),
            pltpu.VMEM((visits - 1,) + piece, jnp.bfloat16),
            pltpu.VMEM((pairs, visits) + tile, jnp.float32),
            pltpu.VMEM((visits, pairs) + tile, jnp.float32),
            pltpu.VMEM((pairs - 1, visits) + tile, jnp.float32),
            pltpu.VMEM((visits,) + tile, jnp.float32),
            pltpu.VMEM((visits - 1,) + tile, jnp.float32),
            pltpu.VMEM((2, TOP, sky_cols), jnp.float32),
            pltpu.VMEM((2, TOP, sky_cols), jnp.float32),
            pltpu.VMEM(piece, jnp.bfloat16),
            pltpu.SemaphoreType.DMA((visits + 1,)),
            sems(visits),
            sems(visits, pairs - 1),
            sems(visits - 1),
            sems(pairs + visits - 1),
            sems(2),
            sems(visits - 1),
            sems(visits, pairs - 1),
            sems(visits, pairs),
        ],
        compiler_params=pltpu.CompilerParams(
            collective_id=0, has_side_effects=True, vmem_limit_bytes=48 * 1024 * 1024
        ),
        name="combine",
    )(
        dense.reshape((visits, pairs, 2) + piece),
        weights.reshape((visits, pairs, 2) + tile),
        threshold_level,
    )
    sky = sky.reshape(sky_rows, sky_cols)

    difference = pl.pallas_call(
        difference_kernel,
        grid_spec=pltpu.PrefetchScalarGridSpec(
            num_scalar_prefetch=2,
            grid=(exposures, tiles),
            in_specs=[
                pl.BlockSpec((1, BLOCK, side), lambda e, p, *_: (e, p, 0)),
                pl.BlockSpec(memory_space=pl.ANY),
            ],
            out_specs=pl.BlockSpec((1, BLOCK, side), lambda e, p, *_: (e, p, 0)),
            scratch_shapes=[
                pltpu.VMEM((exposures, tiles * tiles, BLOCK, BLOCK), jnp.bfloat16),
                pltpu.SemaphoreType.DMA((exposures, tiles * tiles)),
            ],
        ),
        out_shape=jax.ShapeDtypeStruct((exposures, side, side), jnp.float32),
        compiler_params=pltpu.CompilerParams(vmem_limit_bytes=12 * 1024 * 1024),
        name="difference",
    )(owners, dest_column, shifted, sky)
    return (strip, difference)


def solution(mesh):
    placed = (
        P(("visit", "sky"), None, None),
        P(("visit", "sky"), None, None),
        P(("visit", "sky"), None, None),
        P(("visit", "sky"), None, None),
        P(("visit", "sky")),
        P(("visit", "sky"), None, None),
        P(("visit", "sky"), None),
        P(("visit", "sky"), None),
        P(),
    )
    return jax.shard_map(
        shards,
        mesh=mesh,
        in_specs=placed,
        out_specs=(P(("visit", "sky"), None), P(("visit", "sky"), None, None)),
        check_vma=False,
    )
```

time: 264 us -> 95.1 us (0.36)
  waiting for transfers between devices: 160 us -> 0 us
  Pallas kernels: 30.1 us -> 91.8 us
  blocking collectives: 43.1 us -> 0 us
  between operations: 14.3 us -> 0.68 us
  other arithmetic: 8.88 us -> 0 us
  starting transfers between devices: 2.66 us -> 0 us
    reduce_scatter x1 -> x0, waiting for transfers between devices: 99.1 us -> none  [shards(): summed = lax.psum_scatter(dense, axes, scatter_dimension=0, tiled=True)]
    pallas_call x0 -> x1, Pallas kernels: none -> 64.9 us  [shards(): pl.pallas_call(functools.partial(combine_kernel, visits, pairs), in_specs...]
    all_gather x1 -> x0, waiting for transfers between devices: 60.6 us -> none  [shards(): sky = lax.all_gather(strip.astype(jnp.bfloat16), axes, axis=0, tiled=True)]
    all_gather x1 -> x0, blocking collectives: 43.1 us -> none  [shards(): all_weights = lax.all_gather(own_weights, axes)]
    convert_element_type x6 -> x0, other arithmetic: 3.77 us -> none  [the longest x3 2.67 us: bf_values(): return array.astype(jnp.bfloat16).astype(jnp.float32)]
    pallas_call x1, Pallas kernels: 7.8 us -> 4.39 us  [shards(): pl.pallas_call(difference_kernel, grid_spec=pltpu.PrefetchScalarGridSpec(...]
  transfers between devices with their start and end apart: 4 -> 0, of which waited for: 3 -> 0; matrix products, arithmetic and copies ran while one was open for 1% -> 0% of each run, Pallas kernels for 0% -> 0%
where the time goes in v2:
time: 95.1 us; the launch traced here: 94.9 us
  Pallas kernels  91.8 us (97%)
  local copies, waits for them, and re-layouts  2.38 us (3%)
    pallas_call x1, Pallas kernels, shards(): pl.pallas_call(functools.partial(combine_kernel, visits, pairs), in_specs...  64.9 us
    pallas_call x1, Pallas kernels, shards(): pl.pallas_call(conv_kernel, grid_spec=pltpu.PrefetchScalarGridSpec(num_sc...  22.5 us
    pallas_call x1, Pallas kernels, shards(): pl.pallas_call(difference_kernel, grid_spec=pltpu.PrefetchScalarGridSpec(...  4.39 us
    unnamed x10, local copies, waits for them, and re-layouts  2.38 us

profile of v2, /device:TPU:0, one launch (start us, length us, event | category | flops | bytes accessed | tf_op | source)
XLA Modules:
  0.0 94.9 jit_solution(6387426812123592223)
XLA Ops:
  0.6 0.8 copy.11.level_ref
  1.4 22.5 %convolve.1 = (f32[2,512,512]{2,1,0:T(8,128)}, bf16[4096,512]{1,0:T(8,128)(2,1)}, f32[32,8,128]{2,1,0:T(8,128)}) custom-call(s32[2,16]{1,0:T(2,128)} %shift_ref.1, s32[2,16]{1,0:T(2,128)} %bitcast.6, s32[2,16]{1,0:T(2,128)} %column_ref.3, f32[2]{0:T(128)} %weight_ref.1, f32[2,4,16]{2,1,0:T(4,128)} %factor_ref.1, f32[2,512,512]{2,1,0:T(8,128)} %x_ref.1, ...), custom_call_target="tpu_custom_call" | custom-call | tf_op jit(solution)/shard_map/convolve/pallas_call | solution.py:489
  23.9 0.0 copy-start.1
  23.9 0.9 copy-done.1
  24.8 0.0 copy-start
  24.8 0.0 copy-start.2
  24.8 0.0 copy-start.3
  24.8 64.9 %combine.1 = (f32[128,512]{1,0:T(8,128)S(1)}, bf16[4,4,2,128,512]{4,3,2,1,0:T(8,128)(2,1)S(1)}) custom-call(bf16[4,4,2,128,512]{4,3,2,1,0:T(8,128)(2,1)} %bitcast.8, f32[4,4,2,8,128]{4,3,2,1,0:T(8,128)S(1)} %bitcast.5, s32[32,4]{1,0:T(8,128)S(1)} %copy.11.level_ref), custom_call_target="tpu_custom_call" | custom-call | tf_op jit(solution)/shard_map/combine/pallas_call | solution.py:543
  89.7 0.0 copy-done
  89.7 0.0 copy-done.2
  89.7 0.0 copy-done.3
  89.8 4.4 %difference.1 = f32[2,512,512]{2,1,0:T(8,128)} custom-call(s32[2,16]{1,0:T(2,128)S(1)} %bitcast.7, s32[2,16]{1,0:T(2,128)S(1)} %copy-done.3, f32[2,512,512]{2,1,0:T(8,128)S(1)} %copy-done, bf16[4096,512]{1,0:T(8,128)(2,1)S(1)} %bitcast.4), custom_call_target="tpu_custom_call" | custom-call | tf_op jit(solution)/shard_map/difference/pallas_call | solution.py:590
  94.2 0.7 copy.13
Async XLA Ops:
  23.9 0.9 copy-start.1
  24.8 64.9 %copy-start = (f32[2,512,512]{2,1,0:T(8,128)S(1)}, f32[2,512,512]{2,1,0:T(8,128)}, u32[]{:S(2)}) copy-start(f32[2,512,512]{2,1,0:T(8,128)} %get-tuple-element.10.shifted_ref) | copy-start | bytes 6291460
  24.8 64.9 %copy-start.2 = (s32[2,16,1]{1,2,0:T(1,128)S(1)}, s32[2,16,1]{1,2,0:T(1,128)}, u32[]{:S(2)}) copy-start(s32[2,16,1]{1,2,0:T(1,128)} %param.14) | copy-start | bytes 388
  24.8 64.9 %copy-start.3 = (s32[2,16]{1,0:T(2,128)S(1)}, s32[2,16]{1,0:T(2,128)}, u32[]{:S(2)}) copy-start(s32[2,16]{1,0:T(2,128)} %column_ref.3) | copy-start | bytes 388

commit v3 on v2

--- a/solution.py
+++ b/solution.py
@@ -1,4 +1,5 @@
 import functools
+import math
 import jax
 import jax.numpy as jnp
 from jax import lax
@@ -224,6 +225,13 @@
         out_ref[0, :, lanes] = shifted_ref[0, :, lanes] - blocks[exposure, b].astype(jnp.float32)
 
 
+def grid_of(pairs):
+    wide = math.isqrt(pairs)
+    if wide * wide != pairs:
+        wide = pairs
+    return wide, pairs // wide
+
+
 def spline(values, dilation, axis):
     size = values.shape[axis]
     d = dilation
@@ -251,9 +259,12 @@
     level_ref,
     strip_ref,
     sky_ref,
+    held,
     part,
     from_twin,
-    from_plane,
+    from_first,
+    middle,
+    from_second,
     going,
     from_visit,
     w_part,
@@ -266,12 +277,14 @@
     template,
     local_sem,
     twin_sem,
-    plane_sem,
+    first_sem,
+    second_sem,
     visit_sem,
     w_sem,
     halo_sem,
     back_visit_sem,
-    back_plane_sem,
+    back_first_sem,
+    back_second_sem,
     back_twin_sem,
 ):
     z = lax.axis_index("visit")
@@ -292,6 +305,15 @@
     column = [(height, sky) for height in heights]
     ring = [linear(lax.rem(me + devices - 1, devices)), linear(lax.rem(me + 1, devices))]
 
+    wide, tall = grid_of(pairs)
+    y, x = lax.div(p, wide), lax.rem(p, wide)
+    along = [
+        [(z, (y * wide + lax.rem(x + o, wide)) * 2 + core) for o in range(1, wide)],
+        [(z, (lax.rem(y + o, tall) * wide + x) * 2 + core) for o in range(1, tall)],
+    ]
+    sizes, spots = (wide, tall), (x, y)
+    half = strip_ref.shape[1] // 2
+
     everyone = [twin] + plane + column + ring
     barrier = pltpu.get_barrier_semaphore()
     for peer in everyone:
@@ -321,7 +343,7 @@
         across.append(
             send(dense_ref.at[height, :, other], from_twin.at[j], twin_sem, (j,), twin)
         )
-        own = pltpu.make_async_copy(dense_ref.at[height, :, core], part.at[j], local_sem.at[j])
+        own = pltpu.make_async_copy(dense_ref.at[height, :, core], held.at[j], local_sem.at[j])
         own.start()
         local.append(own)
 
@@ -339,22 +361,67 @@
         across[j].wait_recv()
 
         def add(place, carry):
-            part[j, place] = (
-                part[j, place].astype(jnp.float32) + from_twin[j, place].astype(jnp.float32)
+            total = (
+                held[j, place].astype(jnp.float32) + from_twin[j, place].astype(jnp.float32)
             ).astype(jnp.bfloat16)
+            part[j, 0, lax.rem(place, wide) * tall + lax.div(place, wide)] = total[:, :half]
+            part[j, 1, place] = total[:, half:]
             return carry
 
         lax.fori_loop(0, pairs, add, 0)
-        return [
-            send(part.at[j, place], from_plane.at[j, o], plane_sem, (j, o), plane[o])
-            for o, place in enumerate(places)
-        ]
+        copies = []
+        for h in range(2):
+            first, second = sizes[h], sizes[1 - h]
+            for o in range(1, first):
+                at = pl.ds(lax.rem(spots[h] + o, first) * second, second)
+                copies.append(
+                    send(
+                        part.at[j, h, at],
+                        from_first.at[j, h, o - 1],
+                        first_sem,
+                        (j, h, o - 1),
+                        along[h][o - 1],
+                    )
+                )
+        return copies
+
+    def line(j, h, spot):
+        first, second = sizes[h], sizes[1 - h]
+        total = part[j, h, spots[h] * second + spot].astype(jnp.float32)
+        for o in range(first - 1):
+            total = total + from_first[j, h, o, spot].astype(jnp.float32)
+        return total
+
+    def turn(j):
+        copies = []
+        for copy in moves[j]:
+            copy.wait_recv()
+        for h in range(2):
+            second = sizes[1 - h]
+            for o in range(1, second):
+                spot = lax.rem(spots[1 - h] + o, second)
+                middle[j, h, o - 1] = line(j, h, spot).astype(jnp.bfloat16)
+                copies.append(
+                    send(
+                        middle.at[j, h, o - 1],
+                        from_second.at[j, h, o - 1],
+                        second_sem,
+                        (j, h, o - 1),
+                        along[1 - h][o - 1],
+                    )
+                )
+        return copies
 
     def gathered(j):
-        total = part[j, p].astype(jnp.float32)
-        for o in range(pairs - 1):
-            total = total + from_plane[j, o].astype(jnp.float32)
-        return total
+        for copy in turns[j]:
+            copy.wait_recv()
+        halves = []
+        for h in range(2):
+            total = line(j, h, spots[1 - h])
+            for o in range(sizes[1 - h] - 1):
+                total = total + from_second[j, h, o].astype(jnp.float32)
+            halves.append(total)
+        return jnp.concatenate(halves, axis=1)
 
     moves = [spread(0)]
     for copy in w_copies:
@@ -367,15 +434,17 @@
         send(w_going.at[height], w_visit.at[j], w_sem, (pairs + j,), column[j])
         for j, height in enumerate(heights)
     ]
-    climbs = []
-    for j in range(visits):
-        if j + 1 < visits:
-            moves.append(spread(j + 1))
-        for copy in moves[j]:
-            copy.wait_recv()
-        if j + 1 < visits:
-            going[j] = gathered(j).astype(jnp.bfloat16)
-            climbs.append(send(going.at[j], from_visit.at[j], visit_sem, (j,), column[j]))
+    climbs, turns = [], []
+    for j in range(1, visits + 2):
+        if j < visits:
+            moves.append(spread(j))
+        if j <= visits:
+            turns.append(turn(j - 1))
+        if j >= 2:
+            i = j - 2
+            if i < visits - 1:
+                going[i] = gathered(i).astype(jnp.bfloat16)
+                climbs.append(send(going.at[i], from_visit.at[i], visit_sem, (i,), column[i]))
     weight = w_going[z]
     for copy, j in zip(w_copies, range(visits - 1)):
         copy.wait_recv()
@@ -435,29 +504,69 @@
     climbs = [
         send(template, mine, back_visit_sem, (d,), column[d]) for d in range(visits - 1)
     ]
-    spreads, twins = [], []
+    spreads, onward, twins = [], [], []
+
+    def chunk(d, h, row, col):
+        owner = lax.rem(row, tall) * wide + lax.rem(col, wide)
+        return sky_ref.at[
+            lax.rem(z + visits - d, visits), owner, core, :, pl.ds(h * half, half)
+        ]
+
+    def away(d, h, i, o):
+        steps = [(x, y), (y, x)][h]
+        one, two = steps[0] + sizes[h] - i, steps[1] + sizes[1 - h] - o
+        return chunk(d, h, two, one) if h == 0 else chunk(d, h, one, two)
+
+    def second_leg(d, h, i, source, place):
+        onward.append(
+            [
+                (d, h, i, o, send(source, place, back_second_sem, (d, h, i, o - 1), along[1 - h][o - 1]))
+                for o in range(1, sizes[1 - h])
+            ]
+        )
 
     def outward(d):
-        if d == 0:
-            source, place = template, mine
-        else:
+        if d > 0:
             climbs[d - 1].wait_recv()
-            source = place = sky_ref.at[lax.rem(z + visits - d, visits), p, core]
-        spreads.append(
-            [send(source, place, back_plane_sem, (d, o), plane[o]) for o in range(pairs - 1)]
-        )
-        twins.append(send(source, place, back_twin_sem, (d, pairs - 1), twin))
+        batch = []
+        for h in range(2):
+            place = away(d, h, 0, 0)
+            source = template.at[:, pl.ds(h * half, half)] if d == 0 else place
+            for o in range(1, sizes[h]):
+                batch.append(
+                    (h, o, send(source, place, back_first_sem, (d, h, o - 1), along[h][o - 1]))
+                )
+        for h in range(2):
+            place = away(d, h, 0, 0)
+            source = template.at[:, pl.ds(h * half, half)] if d == 0 else place
+            second_leg(d, h, 0, source, place)
+            twins.append(send(source, place, back_twin_sem, (d, h, 0, 0), twin))
+        spreads.append(batch)
+
+    def forward(number):
+        for d, h, i, o, copy in onward[number]:
+            copy.wait_recv()
+            place = away(d, h, i, o)
+            twins.append(send(place, place, back_twin_sem, (d, h, i, o), twin))
 
     outward(0)
+    ready = 0
     for d in range(visits):
         if d + 1 < visits:
             outward(d + 1)
-        for o in range(pairs - 1):
-            spreads[d][o].wait_recv()
-            place = sky_ref.at[
-                lax.rem(z + visits - d, visits), lax.rem(p + pairs - 1 - o, pairs), core
-            ]
-            twins.append(send(place, place, back_twin_sem, (d, o), twin))
+        stop = len(onward)
+        for h, i, copy in spreads[d]:
+            copy.wait_recv()
+            place = away(d, h, i, 0)
+            second_leg(d, h, i, place, place)
+            twins.append(send(place, place, back_twin_sem, (d, h, i, 0), twin))
+        if d > 0:
+            while ready < stop:
+                forward(ready)
+                ready += 1
+    while ready < len(onward):
+        forward(ready)
+        ready += 1
     for copy in twins:
         copy.wait_recv()
     own.wait()
@@ -536,6 +645,8 @@
     vmem = pl.BlockSpec(memory_space=pltpu.VMEM)
     piece = (BLOCK, sky_cols)
     tile = (8, BLOCK)
+    halved = (BLOCK, sky_cols // 2)
+    most, least = max(grid_of(pairs)), min(grid_of(pairs))
 
     def sems(*shape):
         return pltpu.SemaphoreType.DMA((2,) + shape)
@@ -554,8 +665,11 @@
         ],
         scratch_shapes=[
             pltpu.VMEM((visits, pairs) + piece, jnp.bfloat16),
+            pltpu.VMEM((visits, 2, pairs) + halved, jnp.bfloat16),
             pltpu.VMEM((visits, pairs) + piece, jnp.bfloat16),
-            pltpu.VMEM((visits, pairs - 1) + piece, jnp.bfloat16),
+            pltpu.VMEM((visits, 2, most - 1, least) + halved, jnp.bfloat16),
+            pltpu.VMEM((visits, 2, most - 1) + halved, jnp.bfloat16),
+            pltpu.VMEM((visits, 2, most - 1) + halved, jnp.bfloat16),
             pltpu.VMEM((visits - 1,) + piece, jnp.bfloat16),
             pltpu.VMEM((visits - 1,) + piece, jnp.bfloat16),
             pltpu.VMEM((pairs, visits) + tile, jnp.float32),
@@ -568,13 +682,15 @@
             pltpu.VMEM(piece, jnp.bfloat16),
             pltpu.SemaphoreType.DMA((visits + 1,)),
             sems(visits),
-            sems(visits, pairs - 1),
+            sems(visits, 2, most - 1),
+            sems(visits, 2, most - 1),
             sems(visits - 1),
             sems(pairs + visits - 1),
             sems(2),
             sems(visits - 1),
-            sems(visits, pairs - 1),
-            sems(visits, pairs),
+            sems(visits, 2, most - 1),
+            sems(visits, 2, most, most - 1),
+            sems(visits, 2, most, most),
         ],
         compiler_params=pltpu.CompilerParams(
             collective_id=0, has_side_effects=True, vmem_limit_bytes=48 * 1024 * 1024

time: 95.1 us -> 93.1 us (0.979)
  Pallas kernels: 91.8 us -> 89.8 us
    pallas_call x1, Pallas kernels: 64.9 us -> 62.9 us  [shards(): pl.pallas_call(functools.partial(combine_kernel, visits, pairs), in_specs...]
where the time goes in v3:
time: 93.1 us; the launch traced here: 92.8 us
  Pallas kernels  89.8 us (96%)
  local copies, waits for them, and re-layouts  2.38 us (3%)
    pallas_call x1, Pallas kernels, shards(): pl.pallas_call(functools.partial(combine_kernel, visits, pairs), in_specs...  62.9 us
    pallas_call x1, Pallas kernels, shards(): pl.pallas_call(conv_kernel, grid_spec=pltpu.PrefetchScalarGridSpec(num_sc...  22.5 us
    pallas_call x1, Pallas kernels, shards(): pl.pallas_call(difference_kernel, grid_spec=pltpu.PrefetchScalarGridSpec(...  4.39 us
    unnamed x10, local copies, waits for them, and re-layouts  2.38 us

profile of v3, /device:TPU:0, one launch (start us, length us, event | category | flops | bytes accessed | tf_op | source)
XLA Modules:
  0.0 92.8 jit_solution(4799879621776675844)
XLA Ops:
  0.6 0.8 copy.11.level_ref
  1.4 22.5 %convolve.1 = (f32[2,512,512]{2,1,0:T(8,128)}, bf16[4096,512]{1,0:T(8,128)(2,1)}, f32[32,8,128]{2,1,0:T(8,128)}) custom-call(s32[2,16]{1,0:T(2,128)} %shift_ref.1, s32[2,16]{1,0:T(2,128)} %bitcast.6, s32[2,16]{1,0:T(2,128)} %column_ref.3, f32[2]{0:T(128)} %weight_ref.1, f32[2,4,16]{2,1,0:T(4,128)} %factor_ref.1, f32[2,512,512]{2,1,0:T(8,128)} %x_ref.1, ...), custom_call_target="tpu_custom_call" | custom-call | tf_op jit(solution)/shard_map/convolve/pallas_call | solution.py:598
  23.9 0.0 copy-start.1
  23.9 0.9 copy-done.1
  24.8 0.0 copy-start
  24.8 0.0 copy-start.2
  24.8 0.0 copy-start.3
  24.8 62.9 %combine.1 = (f32[128,512]{1,0:T(8,128)S(1)}, bf16[4,4,2,128,512]{4,3,2,1,0:T(8,128)(2,1)S(1)}) custom-call(bf16[4,4,2,128,512]{4,3,2,1,0:T(8,128)(2,1)} %bitcast.8, f32[4,4,2,8,128]{4,3,2,1,0:T(8,128)S(1)} %bitcast.5, s32[32,4]{1,0:T(8,128)S(1)} %copy.11.level_ref), custom_call_target="tpu_custom_call" | custom-call | tf_op jit(solution)/shard_map/combine/pallas_call | solution.py:654
  87.7 0.0 copy-done
  87.7 0.0 copy-done.2
  87.7 0.0 copy-done.3
  87.7 4.4 %difference.1 = f32[2,512,512]{2,1,0:T(8,128)} custom-call(s32[2,16]{1,0:T(2,128)S(1)} %bitcast.7, s32[2,16]{1,0:T(2,128)S(1)} %copy-done.3, f32[2,512,512]{2,1,0:T(8,128)S(1)} %copy-done, bf16[4096,512]{1,0:T(8,128)(2,1)S(1)} %bitcast.4), custom_call_target="tpu_custom_call" | custom-call | tf_op jit(solution)/shard_map/difference/pallas_call | solution.py:706
  92.1 0.7 copy.13
Async XLA Ops:
  23.9 0.9 copy-start.1
  24.8 62.9 %copy-start = (f32[2,512,512]{2,1,0:T(8,128)S(1)}, f32[2,512,512]{2,1,0:T(8,128)}, u32[]{:S(2)}) copy-start(f32[2,512,512]{2,1,0:T(8,128)} %get-tuple-element.10.shifted_ref) | copy-start | bytes 6291460
  24.8 62.9 %copy-start.2 = (s32[2,16,1]{1,2,0:T(1,128)S(1)}, s32[2,16,1]{1,2,0:T(1,128)}, u32[]{:S(2)}) copy-start(s32[2,16,1]{1,2,0:T(1,128)} %param.14) | copy-start | bytes 388
  24.8 62.9 %copy-start.3 = (s32[2,16]{1,0:T(2,128)S(1)}, s32[2,16]{1,0:T(2,128)}, u32[]{:S(2)}) copy-start(s32[2,16]{1,0:T(2,128)} %column_ref.3) | copy-start | bytes 388
